TPU v7x, 32 devices: a whole 2x2x4 slice. The times are simulated.
32 devices in a mesh: section: 2 (over x), expert: 4 (over z), dp: 4 (over y, core).
Axes of the slice: x: 2, y: 2, z: 4, core: 2. Of those that a mesh axis runs over, the one named last changes fastest.
Arguments:
- frames: bfloat16 [4, 32, 48, 1280], P(None, ('expert', 'dp')), may hold values from -6 to 6
- norm_gain: float32 [2, 1280], P('section'), may hold values from 0.1 to 1.9
- router: bfloat16 [2, 1280, 4], P('section'), may hold values from -0.15625 to 0.15625
- w_in: bfloat16 [2, 4, 1280, 256], P('section', 'expert'), may hold values from -0.15625 to 0.15625
- w_out: bfloat16 [2, 4, 256, 1280], P('section', 'expert'), may hold values from -0.375 to 0.375
- routing: int32 [2, 4, 32, 48, 1], P('section', None, ('expert', 'dp')), may hold values from 0 to 3; in each aligned block of 96 rows (0 to 95, 96 to 191, ..., all dimensions but the last counted through in order) at most 27 rows name the same one
- head_gain: float32 [1280], replicated, may hold values from 0.1 to 1.9
- head_weight: bfloat16 [1280, 8000], P(None, 'expert'), may hold values from -6 to 6
- frame_lengths: int32 [4, 32], P(None, ('expert', 'dp')), may hold values from 24 to 48
- labels: int32 [4, 32, 12], P(None, ('expert', 'dp')), may hold values from 1 to 7999
- label_lengths: int32 [4, 32], P(None, ('expert', 'dp')), may hold values from 1 to 12
Outputs:
- losses: float32 [8, 16], P('section', ('expert', 'dp'))
- head_grad: bfloat16 [1280, 8000], P(None, 'expert')
Inputs may be any that keep to these rules, and one draw needn't show every extreme that they name: `routing`: in each layer and micro-batch, within the frames of one device (aligned blocks of 96 frames), no expert is named by more than 27 frames.
All inputs are finite; a program needn't handle non-finite values.
Results may differ from a plain program's by a relative error of at most 0.015.
Values may be sent and summed in bfloat16 or wider, within the bound.
No kernel may reach another device: no remote copies, remote signals or barrier semaphores. Data moves between devices by JAX's collectives and lax.ppermute only.
A program may use at most 64 MiB of HBM per device.

v0:
```python
import jax
import jax.numpy as jnp
import numpy as np
from jax import lax
from jax.experimental import pallas as pl
from jax.experimental.pallas import tpu as pltpu
from jax.sharding import Mesh, PartitionSpec as P

EPSILON = 1e-06
LOG_ZERO = -1e30
VMEM_LIMIT = 24 * 1024 * 1024
LANES = 128
COLS = 16
PEAK, TOTAL, WHOLE = COLS - 3, COLS - 2, COLS - 3
BLOCK_ROWS = 256
NT = (((1,), (1,)), ((), ()))
NN = (((1,), (0,)), ((), ()))


def round_up(value, unit):
    return -(-value // unit) * unit


def vmem_spec():
    return pl.BlockSpec(memory_space=pltpu.VMEM)


def hbm_spec():
    return pl.BlockSpec(memory_space=pltpu.HBM)


def smem_spec():
    return pl.BlockSpec(memory_space=pltpu.SMEM)


def call(kernel, out_shape, flops=0, moved=0, **options):
    return pl.pallas_call(
        kernel,
        out_shape=out_shape,
        compiler_params=pltpu.CompilerParams(vmem_limit_bytes=VMEM_LIMIT),
        cost_estimate=pl.CostEstimate(flops=flops, bytes_accessed=moved, transcendentals=0),
        **options,
    )


def bf16_rows(count, width):
    return jax.ShapeDtypeStruct((count, width), jnp.bfloat16)


def as_mask(values):
    return values.astype(jnp.float32).astype(jnp.bfloat16)


def split_rows(values, out_refs):
    size = out_refs[0].shape[0]
    for turn, out_ref in enumerate(out_refs):
        out_ref[...] = values[turn * size : (turn + 1) * size].astype(jnp.bfloat16)


def join_rows(refs):
    return jnp.concatenate([ref[...].astype(jnp.float32) for ref in refs], axis=0)


def rms_scale(values, gain):
    values = values.astype(jnp.float32)
    scale = lax.rsqrt(jnp.mean(values * values, axis=-1, keepdims=True) + EPSILON)
    return (values * scale * gain).astype(jnp.bfloat16)


def expert_column(ids, frame_count):
    pairs = ids.shape[0]
    square = jnp.concatenate(
        [ids.astype(jnp.float32), jnp.full((LANES - pairs, LANES), -1.0, jnp.float32)], axis=0
    )
    turned = jnp.transpose(square, (1, 0)).astype(jnp.int32)
    return jnp.concatenate([turned[:frame_count, p : p + 1] for p in range(pairs)], axis=0)


def placement(column, member, experts, capacity):
    count = column.shape[0]
    shifted = column - member
    relative = jnp.where(shifted < 0, shifted + experts, shifted)
    lane = lax.broadcasted_iota(jnp.int32, (count, LANES), 1)
    one_hot = (lane == relative).astype(jnp.float32)
    before = lax.broadcasted_iota(jnp.int32, (count, count), 1) <= lax.broadcasted_iota(
        jnp.int32, (count, count), 0
    )
    rank = lax.dot_general(
        as_mask(before), one_hot.astype(jnp.bfloat16), NN, preferred_element_type=jnp.float32
    )
    start = (lane * capacity - 1).astype(jnp.float32)
    slots = jnp.sum(one_hot * (rank + start), axis=1, keepdims=True).astype(jnp.int32)
    places = lax.broadcasted_iota(jnp.int32, (count, experts * capacity), 1)
    return (places == slots).astype(jnp.float32)


def scatter_rows(rows, ids, member, experts, capacity, frame_count, out_refs):
    count = rows.shape[0]
    chosen = placement(expert_column(ids, frame_count), member, experts, capacity)
    tall = round_up(count, LANES)
    if tall > count:
        chosen = jnp.concatenate(
            [chosen, jnp.zeros((tall - count, chosen.shape[1]), jnp.float32)], axis=0
        )
    pick = jnp.transpose(chosen, (1, 0))[:, :count].astype(jnp.bfloat16)
    placed = lax.dot_general(pick, rows, NN, preferred_element_type=jnp.float32)
    split_rows(placed, out_refs)


def combine_rows(rows, returned, ids, table, member, experts, capacity, frame_count):
    column = expert_column(ids, frame_count)
    pick = placement(column, member, experts, capacity).astype(jnp.bfloat16)
    normed = rms_scale(rows, table[:1])
    router = jnp.concatenate(
        [table[8:], jnp.zeros((LANES + 8 - table.shape[0], rows.shape[1]), jnp.float32)], axis=0
    ).astype(jnp.bfloat16)
    logits = lax.dot_general(normed, router, NT, preferred_element_type=jnp.float32)
    lane = lax.broadcasted_iota(jnp.int32, logits.shape, 1)
    gate = jax.nn.sigmoid(jnp.sum(jnp.where(lane == column, logits, 0.0), axis=1, keepdims=True))
    stacked = join_rows(returned).astype(jnp.bfloat16)
    mixed = lax.dot_general(pick, stacked, NN, preferred_element_type=jnp.float32)
    return (rows.astype(jnp.float32) + gate * mixed).astype(jnp.bfloat16)


def dispatch(rows, ids, member, experts, capacity, frame_count):
    width = rows.shape[1]

    def kernel(member_ref, rows_ref, ids_ref, *out_refs):
        scatter_rows(
            rows_ref[...], ids_ref[...], member_ref[0], experts, capacity, frame_count, out_refs
        )

    return call(
        kernel,
        tuple(bf16_rows(capacity, width) for _ in range(experts)),
        1 << 27,
        1 << 20,
        in_specs=[smem_spec()] + [vmem_spec()] * 2,
        out_specs=tuple(vmem_spec() for _ in range(experts)),
    )(member, rows, ids)


def run_expert(received, table, own, other, pick_own):
    count = len(received)
    capacity, width = received[0].shape
    others = len(other)

    def kernel(pick_ref, table_ref, in_ref, out_weight_ref, *refs):
        other_refs, received_refs, out_refs = (
            refs[: 2 * others],
            refs[2 * others : 2 * others + count],
            refs[2 * others + count :],
        )

        def work(pieces):
            normed = rms_scale(join_rows(received_refs), table_ref[:1])
            total = None
            for weight_in, weight_out in pieces:
                hidden = lax.dot_general(
                    normed, weight_in[...], NN, preferred_element_type=jnp.float32
                )
                active = (hidden / (1.0 + jnp.exp(-hidden))).astype(jnp.bfloat16)
                part = lax.dot_general(
                    active, weight_out[...], NN, preferred_element_type=jnp.float32
                )
                total = part if total is None else total + part
            split_rows(total, out_refs)

        if others == 0:
            work([(in_ref, out_weight_ref)])
            return

        @pl.when(pick_ref[0] == 1)
        def _():
            work([(in_ref, out_weight_ref)])

        @pl.when(pick_ref[0] != 1)
        def _():
            work([(other_refs[2 * i], other_refs[2 * i + 1]) for i in range(others)])

    flat = [weight for pair in other for weight in pair]
    return call(
        kernel,
        tuple(bf16_rows(capacity, width) for _ in range(count)),
        4 * count * capacity * width * own[0].shape[1],
        4 << 20,
        in_specs=[smem_spec()] + [vmem_spec()] * (3 + 2 * others + count),
        out_specs=tuple(vmem_spec() for _ in range(count)),
    )(pick_own, table, *own, *flat, *received)


def combine_and_dispatch(
    rows, returned, ids, table, next_ids, member, experts, capacity, frame_count
):
    width = rows.shape[1]

    def kernel(member_ref, rows_ref, ids_ref, table_ref, next_ref, *refs):
        returned_refs, x_ref, out_refs = refs[:experts], refs[experts], refs[experts + 1 :]
        mixed = combine_rows(
            rows_ref[...],
            returned_refs,
            ids_ref[...],
            table_ref[...],
            member_ref[0],
            experts,
            capacity,
            frame_count,
        )
        x_ref[...] = mixed
        scatter_rows(
            mixed, next_ref[...], member_ref[0], experts, capacity, frame_count, out_refs
        )

    shapes = (bf16_rows(*rows.shape),) + tuple(
        bf16_rows(capacity, width) for _ in range(experts)
    )
    result = call(
        kernel,
        shapes,
        1 << 28,
        2 << 20,
        in_specs=[smem_spec()] + [vmem_spec()] * (4 + experts),
        out_specs=tuple(vmem_spec() for _ in shapes),
    )(member, rows, ids, table, next_ids, *returned)
    return result[0], result[1:]


def combine_and_norm(
    rows, returned, ids, table, head_gain, member, experts, capacity, frame_count
):
    def kernel(member_ref, rows_ref, ids_ref, table_ref, head_ref, *refs):
        final = combine_rows(
            rows_ref[...],
            refs[:experts],
            ids_ref[...],
            table_ref[...],
            member_ref[0],
            experts,
            capacity,
            frame_count,
        )
        refs[experts][...] = rms_scale(final, head_ref[...])

    return call(
        kernel,
        bf16_rows(*rows.shape),
        1 << 28,
        2 << 20,
        in_specs=[smem_spec()] + [vmem_spec()] * (4 + experts),
        out_specs=vmem_spec(),
    )(member, rows, ids, table, head_gain, *returned)


def block_list(shard):
    return [(i, min(BLOCK_ROWS, shard - i)) for i in range(0, shard, BLOCK_ROWS)]


def weight_copies(weight_ref, held_ref, sems, shard):
    return [
        pltpu.make_async_copy(
            weight_ref.at[pl.ds(first, size)], held_ref.at[pl.ds(first, size)], sems.at[index]
        )
        for index, (first, size) in enumerate(block_list(shard))
    ]


def label_rows(weight, places):
    shard, width = weight.shape
    entries = places.shape[0]

    def kernel(places_ref, weight_ref, out_ref, held_ref, sems):
        copies = weight_copies(weight_ref, held_ref, sems, shard)
        for copy in copies:
            copy.start()
        total = jnp.zeros((entries, width), jnp.float32)
        for copy, (first, size) in zip(copies, block_list(shard)):
            entry = first + lax.broadcasted_iota(jnp.int32, (entries, size), 1)
            chosen = as_mask(entry == places_ref[...])
            copy.wait()
            total = total + lax.dot_general(
                chosen, held_ref[first : first + size], NN, preferred_element_type=jnp.float32
            )
        out_ref[...] = total.astype(jnp.bfloat16)

    return call(
        kernel,
        bf16_rows(entries, width),
        2 * shard * entries * width,
        6 << 20,
        in_specs=[vmem_spec(), hbm_spec()],
        out_specs=vmem_spec(),
        scratch_shapes=[
            pltpu.VMEM((shard, width), jnp.bfloat16),
            pltpu.SemaphoreType.DMA((len(block_list(shard)),)),
        ],
    )(places, weight)


def head_logits(fill, count, pieces, member, weight, label_weight, frame_count, earlier):
    given = len(pieces)
    ahead = 0 if earlier is None else earlier.shape[0]
    span, width = pieces[0].shape
    row_count = count * span
    shard = weight.shape[0]
    height = round_up(shard, BLOCK_ROWS)
    entries = label_weight.shape[0]
    others = [] if earlier is None else [earlier]

    def kernel(member_ref, weight_ref, label_ref, *refs):
        piece_refs = refs[:given]
        logits_ref, rows_ref, stats_ref, held_ref, sems = refs[given + len(others) :]
        copies = weight_copies(weight_ref, held_ref, sems, shard)
        for copy in copies:
            copy.start()

        def put(slot, piece_ref):
            rows_ref[slot * span : (slot + 1) * span] = piece_ref[...]

        def put_if(condition, slot, piece_ref):
            @pl.when(condition)
            def _():
                put(slot, piece_ref)

        fill(member_ref[0], piece_refs, put, put_if)
        peak = jnp.full((1, row_count), LOG_ZERO, jnp.float32)
        total = jnp.zeros((1, row_count), jnp.float32)
        for copy, (first, size) in zip(copies, block_list(shard)):
            copy.wait()
            logits = lax.dot_general(
                held_ref[first : first + size],
                rows_ref[...],
                NT,
                preferred_element_type=jnp.float32,
            )
            logits_ref[first : first + size] = logits
            before = peak
            peak = jnp.maximum(before, jnp.max(logits, axis=0, keepdims=True))
            total = total * jnp.exp(before - peak) + jnp.sum(
                jnp.exp(logits - peak), axis=0, keepdims=True
            )
        if height > shard:
            logits_ref[shard:] = jnp.full((height - shard, row_count), LOG_ZERO, jnp.float32)
        crossed = lax.dot_general(
            label_ref[...], rows_ref[...], NT, preferred_element_type=jnp.float32
        )
        owner = lax.broadcasted_iota(jnp.int32, (COLS, row_count), 1) // frame_count
        picked = jnp.zeros((COLS, row_count), jnp.float32)
        for utterance in range(entries // COLS):
            part = crossed[utterance * COLS : (utterance + 1) * COLS]
            picked = picked + jnp.where(owner == utterance, part, 0.0)
        place = lax.broadcasted_iota(jnp.int32, (COLS, row_count), 0)
        stats = jnp.where(place == PEAK, peak, picked)
        stats = jnp.where(place == TOTAL, total, stats)
        for slot in range(ahead):
            stats_ref[slot] = refs[given][slot]
        for slot in range(count):
            stats_ref[ahead + slot] = stats[:, slot * span : (slot + 1) * span]

    return call(
        kernel,
        (
            jax.ShapeDtypeStruct((height, row_count), jnp.float32),
            bf16_rows(row_count, width),
            jax.ShapeDtypeStruct((ahead + count, COLS, span), jnp.float32),
        ),
        2 * height * row_count * width,
        9 << 20,
        in_specs=[smem_spec(), hbm_spec()] + [vmem_spec()] * (1 + given + len(others)),
        out_specs=tuple(vmem_spec() for _ in range(3)),
        scratch_shapes=[
            pltpu.VMEM((shard, width), jnp.bfloat16),
            pltpu.SemaphoreType.DMA((len(block_list(shard)),)),
        ],
    )(member, weight, label_weight, *pieces, *others)


def fill_near(place, piece_refs, put, put_if):
    value_ref, left_ref, right_ref = piece_refs
    put(0, value_ref)
    put_if(place < 2, 1, left_ref)
    put_if(place >= 2, 1, right_ref)


def fill_far(place, piece_refs, put, put_if):
    far_ref, end_ref, left_ref, right_ref = piece_refs
    put(0, far_ref)
    put_if((place == 0) | (place == 3), 1, end_ref)
    put_if(place == 1, 1, right_ref)
    put_if(place == 2, 1, left_ref)


def fill_all(place, piece_refs, put, put_if):
    for slot, piece_ref in enumerate(piece_refs):
        put(slot, piece_ref)


def log_add(first, second):
    peak = jnp.maximum(first, second)
    return peak + jnp.log(jnp.exp(first - peak) + jnp.exp(second - peak))


def log_add3(first, second, third):
    peak = jnp.maximum(jnp.maximum(first, second), third)
    return peak + jnp.log(
        jnp.exp(first - peak) + jnp.exp(second - peak) + jnp.exp(third - peak)
    )


def ctc_pass(stats, slots, labels, frame_counts, label_counts, frame_count, label_max):
    sources = len(stats)
    count, _, span = stats[0].shape
    row_count = count * span
    utterances = labels.shape[0]
    entries = utterances * COLS
    tall = round_up(span, LANES)

    def kernel(slots_ref, labels_ref, frames_ref, counts_ref, *refs):
        (
            out_ref,
            high_ref,
            low_ref,
            loss_ref,
            turn_ref,
            emission_ref,
            emit_blank,
            emit_label,
            blank_fwd,
            label_fwd,
            blank_bwd,
            label_bwd,
            occupancy_ref,
        ) = refs[sources:]
        place = lax.broadcasted_iota(jnp.int32, (COLS, span), 0)
        turn_ref[...] = jnp.zeros(turn_ref.shape, jnp.float32)
        for slot in range(count):
            found = [refs[k][slots_ref[k * count + slot]] for k in range(sources)]
            joined = found[0]
            peak = found[0][PEAK : PEAK + 1]
            for other in found[1:]:
                joined = joined + other
                peak = jnp.maximum(peak, other[PEAK : PEAK + 1])
            total = jnp.zeros((1, span), jnp.float32)
            for other in found:
                total = total + other[TOTAL : TOTAL + 1] * jnp.exp(other[PEAK : PEAK + 1] - peak)
            log_total = peak + jnp.log(total)
            turn_ref[:COLS, :span] = jnp.where(place == TOTAL, log_total, joined - log_total)
            emission_ref[slot * span : (slot + 1) * span] = jnp.transpose(turn_ref[...], (1, 0))[
                :span
            ]

        lane = lax.broadcasted_iota(jnp.int32, (utterances, LANES), 1)
        is_label = lane < label_max
        is_blank = lane <= label_max
        names = labels_ref[...]
        earlier = pltpu.roll(names, 1, 1)
        skip = is_label & (lane >= 1) & (names != 0) & (names != earlier)
        later = pltpu.roll(names, LANES - 1, 1)
        skip_next = (lane < label_max - 1) & (later != 0) & (later != names)
        frames = frames_ref[...]
        counts = counts_ref[...]
        ends_blank = jnp.where(lane == counts, 0.0, LOG_ZERO)
        ends_label = jnp.where(lane == counts - 1, 0.0, LOG_ZERO)

        def spread(step, carry):
            row = emission_ref[pl.ds(step, utterances, stride=frame_count), :]
            blank = jnp.sum(jnp.where(lane == label_max, row, 0.0), axis=1, keepdims=True)
            emit_blank[step] = jnp.where(is_blank, blank, LOG_ZERO)
            emit_label[step] = jnp.where(is_label, row, LOG_ZERO)
            return carry

        lax.fori_loop(0, frame_count, spread, 0, unroll=16)

        def advance(step, carry):
            fwd_blank, fwd_label, bwd_blank, bwd_label = carry
            moved = jnp.where(lane == 0, LOG_ZERO, pltpu.roll(fwd_label, 1, 1))
            new_blank = log_add(fwd_blank, moved) + emit_blank[step]
            new_label = (
                log_add3(fwd_label, fwd_blank, jnp.where(skip, moved, LOG_ZERO))
                + emit_label[step]
            )
            alive = step < frames
            fwd_blank = jnp.where(alive, new_blank, fwd_blank)
            fwd_label = jnp.where(alive, new_label, fwd_label)
            blank_fwd[step] = fwd_blank
            label_fwd[step] = fwd_label

            back = frame_count - 1 - step
            out_blank = bwd_blank + emit_blank[back + 1]
            out_label = bwd_label + emit_label[back + 1]
            next_blank = pltpu.roll(out_blank, LANES - 1, 1)
            next_label = jnp.where(skip_next, pltpu.roll(out_label, LANES - 1, 1), LOG_ZERO)
            ended = back >= frames - 1
            bwd_blank = jnp.where(ended, ends_blank, log_add(out_blank, out_label))
            bwd_label = jnp.where(
                ended, ends_label, log_add3(out_label, next_blank, next_label)
            )
            blank_bwd[back] = bwd_blank
            label_bwd[back] = bwd_label
            return (fwd_blank, fwd_label, bwd_blank, bwd_label)

        first_blank = jnp.where(lane == 0, emit_blank[0], LOG_ZERO)
        first_label = jnp.where(lane == 0, emit_label[0], LOG_ZERO)
        blank_fwd[0] = first_blank
        label_fwd[0] = first_label
        blank_bwd[frame_count - 1] = ends_blank
        label_bwd[frame_count - 1] = ends_label
        fwd_blank, fwd_label, _, _ = lax.fori_loop(
            1, frame_count, advance, (first_blank, first_label, ends_blank, ends_label), unroll=4
        )
        end_state = jnp.sum(jnp.where(lane == counts, fwd_blank, 0.0), axis=1, keepdims=True)
        near_state = jnp.sum(jnp.where(lane == counts - 1, fwd_label, 0.0), axis=1, keepdims=True)
        log_like = log_add(end_state, near_state)
        loss_ref[...] = jnp.broadcast_to(-log_like, (utterances, LANES))

        def occupy(step, carry):
            blank = jnp.exp(blank_fwd[step] + blank_bwd[step] - log_like)
            label = jnp.exp(label_fwd[step] + label_bwd[step] - log_like)
            blank = jnp.sum(jnp.where(is_blank, blank, 0.0), axis=1, keepdims=True)
            label = jnp.where(is_label, label, 0.0)
            whole = blank + jnp.sum(label, axis=1, keepdims=True)
            filled = jnp.where(lane == label_max, blank, label)
            filled = jnp.where(lane == WHOLE, whole, filled)
            filled = jnp.where(step < frames, -filled, 0.0)
            row = emission_ref[pl.ds(step, utterances, stride=frame_count), :]
            occupancy_ref[pl.ds(step, utterances, stride=frame_count), :] = jnp.where(
                lane == TOTAL, row, filled
            )
            return carry

        lax.fori_loop(0, frame_count, occupy, 0, unroll=16)
        turned = jnp.transpose(occupancy_ref[...], (1, 0))[:COLS]
        out_ref[...] = turned
        row_place = lax.broadcasted_iota(jnp.int32, (COLS, row_count), 0)
        owner = lax.broadcasted_iota(jnp.int32, (COLS, row_count), 1) // frame_count
        source = jnp.where(row_place < WHOLE, turned, 0.0)
        for utterance in range(utterances):
            part = jnp.where(owner == utterance, source, 0.0)
            high = part.astype(jnp.bfloat16)
            high_ref[utterance * COLS : (utterance + 1) * COLS] = high
            low_ref[utterance * COLS : (utterance + 1) * COLS] = (
                part - high.astype(jnp.float32)
            ).astype(jnp.bfloat16)

    held = pltpu.VMEM((frame_count, utterances, LANES), jnp.float32)
    table = pltpu.VMEM((row_count, LANES), jnp.float32)
    return call(
        kernel,
        (
            jax.ShapeDtypeStruct((COLS, row_count), jnp.float32),
            bf16_rows(entries, row_count),
            bf16_rows(entries, row_count),
            jax.ShapeDtypeStruct((utterances, LANES), jnp.float32),
        ),
        1 << 26,
        1 << 20,
        in_specs=[smem_spec()] + [vmem_spec()] * (3 + sources),
        out_specs=tuple(vmem_spec() for _ in range(4)),
        scratch_shapes=[pltpu.VMEM((LANES, tall), jnp.float32), table]
        + [held] * 6
        + [table],
    )(slots, labels, frame_counts, label_counts, *stats)


def head_gradient(logits, rows, occupancy, high, low, places, order, outputs, each):
    count = len(logits)
    row_count, width = rows[0].shape
    entries = places.shape[1]
    blocks = outputs * each

    def kernel(order_ref, *refs):
        logits_refs, rows_refs = refs[:count], refs[count : 2 * count]
        occupancy_ref, high_ref, low_ref, places_ref = refs[2 * count : 2 * count + 4]
        out_refs = refs[2 * count + 4 :]
        for block in range(blocks):
            start = pl.multiple_of(order_ref[block] * BLOCK_ROWS, BLOCK_ROWS)
            entry = start + lax.broadcasted_iota(jnp.int32, (BLOCK_ROWS, entries), 0)
            select = as_mask(entry == places_ref[...])
            total = None
            for g in range(count):
                lanes = slice(g * row_count, (g + 1) * row_count)
                scattered = lax.dot_general(
                    select, high_ref[:, lanes], NN, preferred_element_type=jnp.float32
                ) + lax.dot_general(
                    select, low_ref[:, lanes], NN, preferred_element_type=jnp.float32
                )
                whole = occupancy_ref[WHOLE : WHOLE + 1, lanes]
                log_total = occupancy_ref[TOTAL : TOTAL + 1, lanes]
                values = logits_refs[g][pl.ds(start, BLOCK_ROWS), :]
                grad = (scattered - jnp.exp(values - log_total) * whole).astype(jnp.bfloat16)
                part = lax.dot_general(
                    grad, rows_refs[g][...], NN, preferred_element_type=jnp.float32
                )
                total = part if total is None else total + part
            out_refs[block // each][
                block % each * BLOCK_ROWS : (block % each + 1) * BLOCK_ROWS
            ] = total.astype(jnp.bfloat16)

    return call(
        kernel,
        tuple(bf16_rows(each * BLOCK_ROWS, width) for _ in range(outputs)),
        2 * blocks * BLOCK_ROWS * count * row_count * (width + 2 * entries),
        10 << 20,
        in_specs=[smem_spec()] + [vmem_spec()] * (2 * count + 4),
        out_specs=tuple(vmem_spec() for _ in range(outputs)),
    )(order, *logits, *rows, occupancy, high, low, places)


def assemble(pieces, offsets, height):
    count = len(pieces)
    part, width = pieces[0].shape
    short = height % part

    def kernel(offsets_ref, *refs):
        out_ref, sems = refs[count], refs[count + 1]

        def each(act):
            for index in range(count):
                offset = pl.multiple_of(offsets_ref[index], part)

                @pl.when(offset + part <= height)
                def _():
                    act(
                        pltpu.make_async_copy(
                            refs[index], out_ref.at[pl.ds(offset, part)], sems.at[index]
                        )
                    )

                if short:

                    @pl.when(offset + part > height)
                    def _():
                        act(
                            pltpu.make_async_copy(
                                refs[index].at[pl.ds(0, short)],
                                out_ref.at[pl.ds(height - short, short)],
                                sems.at[index],
                            )
                        )

        each(lambda copy: copy.start())
        each(lambda copy: copy.wait())

    return call(
        kernel,
        bf16_rows(height, width),
        0,
        2 * height * width * 2,
        in_specs=[smem_spec()] + [pl.BlockSpec(memory_space=pl.ANY)] * count,
        out_specs=pl.BlockSpec(memory_space=pl.ANY),
        scratch_shapes=[pltpu.SemaphoreType.DMA((count,))],
    )(offsets, *pieces)


def swap(value, axis):
    return lax.ppermute(value, axis, [(0, 1), (1, 0)])


def rotate(value, axis, by):
    count = lax.axis_size(axis)
    return lax.ppermute(value, axis, [(i, (i + by) % count) for i in range(count)])


def after(value, *others):
    return lax.optimization_barrier((value,) + others)[0]


def line_near(value):
    left = lax.ppermute(value, "expert", [(1, 0), (2, 1), (3, 2)])
    right = lax.ppermute(value, "expert", [(0, 1), (1, 2), (2, 3)])
    return left, right


def line_far(near, member):
    left = lax.ppermute(near[0], "expert", [(1, 0), (2, 1)])
    right = lax.ppermute(near[1], "expert", [(1, 2), (2, 3)])
    return jnp.where(member < 2, left, right)


def line_end(far):
    return lax.ppermute(far, "expert", [(1, 0), (2, 3)])


LINE_ORDER = np.array([[0, 1, 2, 3], [1, 2, 3, 0], [2, 1, 0, 3], [3, 2, 1, 0]])


def slot_orders(count):
    return LINE_ORDER if count == 4 else np.tile(np.arange(count), (count, 1))


def slot_tables(count):
    orders = slot_orders(count)
    tables = np.zeros((count, count, count), np.int32)
    for member in range(count):
        for k in range(count):
            source = (member + k) % count
            for slot in range(count):
                tables[member, k, slot] = list(orders[source]).index(orders[member][slot])
    return tables.reshape(count, count * count)


def add(first, second):
    return (first.astype(jnp.float32) + second.astype(jnp.float32)).astype(jnp.bfloat16)


def per_device(
    frames,
    norm_gain,
    router,
    w_in,
    w_out,
    routing,
    head_gain,
    head_weight,
    frame_lengths,
    labels,
    label_lengths,
):
    sections = lax.axis_size("section")
    section_id = lax.axis_index("section")
    group_size = lax.axis_size("expert")
    member = lax.axis_index("expert")
    outer_size = lax.axis_size("dpo")
    inner_size = lax.axis_size("dpi")
    core = lax.axis_index("dpi")
    micro, utt_dev, frame_count, width = frames.shape
    label_max = labels.shape[2]
    experts = w_in.shape[1] * group_size
    hidden = w_in.shape[3]
    pair_count = micro * utt_dev
    per_section = pair_count // sections
    first_pair = section_id * per_section
    share = (utt_dev * frame_count * 9 + 8 * experts - 1) // (8 * experts)
    capacity = round_up(share * -(-per_section // utt_dev), 8)
    span = per_section * frame_count
    member_ref = member.astype(jnp.int32).reshape(1)

    def mine_of(value):
        return lax.dynamic_slice_in_dim(value, first_pair, per_section, 0)

    def exchange(blocks, sign):
        return [blocks[0]] + [
            rotate(blocks[k], "expert", sign * k) for k in range(1, group_size)
        ]

    def lanes_of(ids):
        return jnp.pad(mine_of(ids), ((0, 0), (0, LANES - frame_count)), constant_values=-1)

    current = lax.dynamic_slice_in_dim(
        frames.reshape(pair_count * frame_count, width), first_pair * frame_count, span, 0
    )
    own_ids = routing.reshape(pair_count, frame_count)
    paired = sections == 2 and inner_size == 2
    if paired:
        other_ids = swap(own_ids, "section")
        all_ids = [
            jnp.where(section_id == layer, own_ids, other_ids) for layer in range(sections)
        ]
    else:
        all_ids = lax.all_gather(own_ids, "section")
    layer_ids = [lanes_of(all_ids[layer]) for layer in range(sections)]
    outgoing = dispatch(current, layer_ids[0], member_ref, experts, capacity, frame_count)
    received = exchange(outgoing, 1)

    own_table = jnp.concatenate(
        [
            norm_gain,
            jnp.zeros((7, width), jnp.float32),
            jnp.transpose(router[0]).astype(jnp.float32),
            jnp.zeros((round_up(experts, 8) - experts, width), jnp.float32),
        ],
        axis=0,
    )
    own = (w_in[0, 0], w_out[0, 0])
    if paired:
        other_table = swap(own_table, "section")
        half = hidden // 2
        sent_in = lax.dynamic_slice(own[0], (0, core * half), (width, half))
        sent_out = lax.dynamic_slice(own[1], (core * half, 0), (half, width))
        sent_in, sent_out = lax.optimization_barrier((sent_in, sent_out, own_table))[:2]
        came_in = swap(sent_in, "section")
        came_out = swap(sent_out, "section")
        other = [(came_in, came_out), (swap(came_in, "dpi"), swap(came_out, "dpi"))]
    else:
        all_tables = lax.all_gather(own_table, "section")
        all_in = lax.all_gather(own[0], "section")
        all_out = lax.all_gather(own[1], "section")

    layers = []
    for layer in range(sections):
        if paired:
            mine = section_id == layer
            table = jnp.where(mine, own_table, other_table)
            layers.append((table, own, other, mine.astype(jnp.int32).reshape(1)))
        else:
            chosen = (all_in[layer], all_out[layer])
            layers.append((all_tables[layer], chosen, [], jnp.ones((1,), jnp.int32)))

    labels, frame_lengths, label_lengths = lax.optimization_barrier(
        (labels, frame_lengths, label_lengths, outgoing[0])
    )[:3]
    notes = jnp.concatenate(
        [
            mine_of(labels.reshape(pair_count, label_max)),
            mine_of(frame_lengths.reshape(pair_count, 1)),
            mine_of(label_lengths.reshape(pair_count, 1)),
        ],
        axis=1,
    )
    if group_size == 4:
        found = [notes] + [rotate(notes, "expert", -k) for k in range(1, group_size)]
        low = member < 2
        notes_all = jnp.stack(
            [
                found[0],
                jnp.where(low, found[1], found[3]),
                found[2],
                jnp.where(low, found[3], found[1]),
            ]
        )
    else:
        notes_all = lax.all_gather(notes, "expert")
    shard = head_weight.shape[1]
    weight_rows = jnp.transpose(head_weight)
    notes_all = notes_all.reshape(-1, label_max + 2)
    utterances = notes_all.shape[0]
    names = notes_all[:, :label_max]
    named = jnp.concatenate(
        [
            names,
            jnp.zeros((utterances, 1), jnp.int32),
            jnp.full((utterances, COLS - label_max - 1), -1, jnp.int32),
        ],
        axis=1,
    ).reshape(utterances * COLS)
    local = named - member * shard
    places = jnp.where((named >= 0) & (local >= 0) & (local < shard), local, -1)
    label_weight = label_rows(weight_rows, places.reshape(-1, 1))
    received, label_weight = lax.optimization_barrier((received, label_weight))
    slot_entries = per_section * COLS

    for layer in range(sections):
        table, weights, others, pick_own = layers[layer]
        done = run_expert(received, table, weights, others, pick_own)
        returned = exchange(done, -1)
        if layer < sections - 1:
            current, outgoing = combine_and_dispatch(
                current,
                returned,
                layer_ids[layer],
                table,
                layer_ids[layer + 1],
                member_ref,
                experts,
                capacity,
                frame_count,
            )
            received = exchange(outgoing, 1)
        else:
            normed = combine_and_norm(
                current,
                returned,
                layer_ids[layer],
                table,
                head_gain.reshape(1, width),
                member_ref,
                experts,
                capacity,
                frame_count,
            )

    def logits_of(fill, first, count, pieces, earlier):
        chosen = label_weight[first * slot_entries : (first + count) * slot_entries]
        return head_logits(
            fill, count, pieces, member_ref, weight_rows, chosen, frame_count, earlier
        )

    if group_size == 4:
        left, right = line_near(normed)
        far = line_far((left, right), member)
        end = line_end(far)
        heads = [logits_of(fill_near, 0, 2, [normed, left, right], None)]
        heads.append(logits_of(fill_far, 2, 2, [far, end, left, right], heads[0][2]))
        stats = heads[1][2]
        found = [stats] + [rotate(stats, "expert", -k) for k in range(1, group_size)]
    else:
        gathered = lax.all_gather(normed, "expert")
        pieces = [gathered[k] for k in range(group_size)]
        heads = [logits_of(fill_all, 0, group_size, pieces, None)]
        gathered = lax.all_gather(heads[0][2], "expert")
        found = [
            lax.dynamic_index_in_dim(gathered, (member + k) % group_size, 0, keepdims=False)
            for k in range(group_size)
        ]
    tables = jnp.asarray(slot_tables(group_size))
    slots = lax.dynamic_index_in_dim(tables, member, 0, keepdims=False)
    occupancy, high, low, losses = ctc_pass(
        found,
        slots,
        jnp.pad(names, ((0, 0), (0, LANES - label_max))),
        notes_all[:, label_max : label_max + 1],
        notes_all[:, label_max + 1 :],
        frame_count,
        label_max,
    )
    own_slot = 0 if group_size == 4 else member
    my_losses = lax.dynamic_slice(losses, (own_slot * per_section, 0), (per_section, 1))

    def gradient(order, outputs, each):
        return head_gradient(
            [head[0] for head in heads],
            [head[1] for head in heads],
            occupancy,
            high,
            low,
            places.reshape(1, -1),
            order,
            outputs,
            each,
        )

    blocks = heads[0][0].shape[0] // BLOCK_ROWS
    if paired and outer_size == 2 and blocks == 8:
        outer = lax.axis_index("dpo")

        def pair_of(side, first, second):
            return jnp.stack([side * 4 + first, side * 4 + 2 + second]).astype(jnp.int32)

        came_sent = swap(
            gradient(pair_of(1 - core, 1 - section_id, 1 - outer), 1, 2)[0], "dpi"
        )
        sent = add(gradient(pair_of(core, 1 - section_id, 1 - outer), 1, 2)[0], came_sent)
        first_in = swap(sent[:BLOCK_ROWS], "section")
        second_in = swap(sent[BLOCK_ROWS:], "dpo")
        order = jnp.concatenate(
            [pair_of(1 - core, section_id, outer), pair_of(core, section_id, outer)]
        )
        sibling_kept, own_kept = gradient(after(order, sent), 2, 2)
        kept = add(own_kept, swap(sibling_kept, "dpi"))
        first = add(kept[:BLOCK_ROWS], first_in)
        second = add(kept[BLOCK_ROWS:], second_in)
        part = BLOCK_ROWS // 2

        def piece(value, index):
            return lax.dynamic_slice_in_dim(value, index * part, part, 0)

        first_far = swap(piece(first, 1 - outer), "dpo")
        second_far = swap(piece(second, 1 - section_id), "section")
        final = jnp.concatenate(
            [add(piece(first, outer), first_far), add(piece(second, section_id), second_far)],
            axis=0,
        )
        across = swap(final, "section")
        beside = swap(final, "dpo")
        first_diagonal = swap(beside[:part], "section")
        second_diagonal = swap(across[part:], "dpo")
        mine = [final, across, beside, first_diagonal, second_diagonal]
        theirs = [swap(value, "dpi") for value in mine]
        pieces, offsets = [], []
        for side, held in ((core, mine), (1 - core, theirs)):
            where = (
                (section_id, outer),
                (1 - section_id, outer),
                (section_id, 1 - outer),
            )
            for value, (s, y) in zip(held[:3], where):
                pieces += [value[:part], value[part:]]
                offsets += [
                    side * 1024 + s * 256 + y * 128,
                    side * 1024 + 512 + y * 256 + s * 128,
                ]
            pieces += held[3:]
            s, y = 1 - section_id, 1 - outer
            offsets += [
                side * 1024 + s * 256 + y * 128,
                side * 1024 + 512 + y * 256 + s * 128,
            ]
        whole = assemble(pieces, jnp.stack(offsets).astype(jnp.int32), shard)
    else:
        partial = gradient(jnp.arange(blocks, dtype=jnp.int32), 1, blocks)[0][:shard]
        whole = lax.psum(partial.astype(jnp.float32), ("section", "dpo", "dpi")).astype(
            jnp.bfloat16
        )
    return (my_losses, jnp.transpose(whole))


def solution(mesh):
    sections, group_size, spread = (mesh.shape[name] for name in ("section", "expert", "dp"))
    inner = 2 if spread % 2 == 0 else 1
    split = Mesh(
        mesh.devices.reshape(sections, group_size, spread // inner, inner),
        ("section", "expert", "dpo", "dpi"),
    )
    block = ("expert", "dpo", "dpi")
    placed = (
        P(None, block, None, None),
        P("section", None),
        P("section", None, None),
        P("section", "expert", None, None),
        P("section", "expert", None, None),
        P("section", None, block, None, None),
        P(),
        P(None, "expert"),
        P(None, block),
        P(None, block, None),
        P(None, block),
    )
    return jax.shard_map(
        per_device,
        mesh=split,
        in_specs=placed,
        out_specs=(P("section", block), P(None, "expert")),
        check_vma=False,
    )
```

profile of v0, /device:TPU:0, one launch (start us, length us, event | category | flops | bytes accessed | tf_op | source)
XLA Modules:
  0.0 245.2 jit_solution(15854032658875737036)
XLA Ops:
  0.7 3.0 %collective-permute-start = (s32[8,48]{1,0:T(8,128)}, s32[8,48]{1,0:T(8,128)S(1)}, u32[]{:S(2)}, u32[]{:S(2)}) collective-permute-start(s32[8,48]{1,0:T(8,128)} %bitcast.68), channel_id=1, source_target_pairs={{0,16},{16,0},{1,17},{17,1},{2,18},{18,2},{3,19},{19,3},{4,20},{20... | collective-permute-start | bytes 4616 | tf_op jit(solution)/shard_map/ppermute | solution.py:655
  15.5 4.1 %collective-permute-start.1 = (s32[4,14]{1,0:T(4,128)S(1)}, s32[4,14]{1,0:T(4,128)S(1)}, u32[]{:S(2)}, u32[]{:S(2)}) collective-permute-start(s32[4,14]{1,0:T(4,128)S(1)} %pad_add_fusion.1), channel_id=1, source_target_pairs={{0,12},{4,0},{8,4},{12,8},{1,13},{5,1},{9,5},{13,9},{2,14},{6,2},{... | collective-permute-start | bytes 680 | tf_op jit(solution)/shard_map/ppermute | solution.py:660
  22.1 2.8 %collective-permute-done.2 = s32[4,14]{1,0:T(4,128)S(1)} collective-permute-done((s32[4,14]{1,0:T(4,128)S(1)}, s32[4,14]{1,0:T(4,128)S(1)}, u32[]{:S(2)}, u32[]{:S(2)}) %collective-permute-start.2) | collective-permute-done | bytes 256 | tf_op jit(solution)/shard_map/ppermute | solution.py:660
  26.9 2.4 copy-done.5
  29.4 4.0 %shard_map.132 = bf16[256,1280]{1,0:T(8,128)(2,1)S(1)} custom-call(s32[256,1]{1,0:T(8,128)S(1)} %and_select_fusion.places_ref, bf16[2000,1280]{1,0:T(8,128)(2,1)S(1)} %bitcast.56), custom_call_target="tpu_custom_call" | custom-call | flops 1310720000 | bytes 6291456 | tf_op jit(solution)/shard_map/pallas_call | solution.py:285
  33.5 3.1 %collective-permute-start.6 = (bf16[56,1280]{1,0:T(8,128)(2,1)S(1)}, bf16[56,1280]{1,0:T(8,128)(2,1)S(1)}, u32[]{:S(2)}, u32[]{:S(2)}) collective-permute-start(bf16[56,1280]{1,0:T(8,128)(2,1)S(1)} %copy-done.29), channel_id=1, source_target_pairs={{0,12},{4,0},{8,4},{12,8},{1,13},{5,1},{9,5},{13,9},{2,14},{6,2},{... | collective-permute-start | bytes 430088 | tf_op jit(solution)/shard_map/ppermute | solution.py:660
  42.6 3.3 %collective-permute-start.12 = (bf16[56,1280]{1,0:T(8,128)(2,1)S(1)}, bf16[56,1280]{1,0:T(8,128)(2,1)S(1)}, u32[]{:S(2)}, u32[]{:S(2)}) collective-permute-start(bf16[56,1280]{1,0:T(8,128)(2,1)S(1)} %get-tuple-element.57), channel_id=1, source_target_pairs={{0,12},{4,0},{8,4},{12,8},{1,13},{5,1},{9,5},{13,9},{2,14},{6,2},{... | collective-permute-start | bytes 430088 | tf_op jit(solution)/shard_map/ppermute | solution.py:660
  48.8 7.7 %collective-permute-done.13.refs_2_ = bf16[56,1280]{1,0:T(8,128)(2,1)S(1)} collective-permute-done((bf16[56,1280]{1,0:T(8,128)(2,1)S(1)}, bf16[56,1280]{1,0:T(8,128)(2,1)S(1)}, u32[]{:S(2)}, u32[]{:S(2)}) %collective-permute-start.13) | collective-permute-done | bytes 143392 | tf_op jit(solution)/shard_map/ppermute | solution.py:660
  61.2 2.9 %collective-permute-start.17 = (bf16[56,1280]{1,0:T(8,128)(2,1)}, bf16[56,1280]{1,0:T(8,128)(2,1)S(1)}, u32[]{:S(2)}, u32[]{:S(2)}) collective-permute-start(bf16[56,1280]{1,0:T(8,128)(2,1)} %get-tuple-element.64), channel_id=1, source_target_pairs={{0,12},{4,0},{8,4},{12,8},{1,13},{5,1},{9,5},{13,9},{2,14},{6,2},{... | collective-permute-start | bytes 430088 | tf_op jit(solution)/shard_map/ppermute | solution.py:660
  64.1 4.2 %collective-permute-done.15.refs_5_ = bf16[56,1280]{1,0:T(8,128)(2,1)S(1)} collective-permute-done((bf16[56,1280]{1,0:T(8,128)(2,1)}, bf16[56,1280]{1,0:T(8,128)(2,1)S(1)}, u32[]{:S(2)}, u32[]{:S(2)}) %collective-permute-start.15) | collective-permute-done | bytes 143392 | tf_op jit(solution)/shard_map/ppermute | solution.py:660
  68.3 2.9 %collective-permute-done.16.refs_6_ = bf16[56,1280]{1,0:T(8,128)(2,1)S(1)} collective-permute-done((bf16[56,1280]{1,0:T(8,128)(2,1)}, bf16[56,1280]{1,0:T(8,128)(2,1)S(1)}, u32[]{:S(2)}, u32[]{:S(2)}) %collective-permute-start.16) | collective-permute-done | bytes 143392 | tf_op jit(solution)/shard_map/ppermute | solution.py:660
  76.3 5.0 %collective-permute-start.18 = (bf16[56,1280]{1,0:T(8,128)(2,1)S(1)}, bf16[56,1280]{1,0:T(8,128)(2,1)S(1)}, u32[]{:S(2)}, u32[]{:S(2)}) collective-permute-start(bf16[56,1280]{1,0:T(8,128)(2,1)S(1)} %get-tuple-element.66), channel_id=1, source_target_pairs={{0,12},{4,0},{8,4},{12,8},{1,13},{5,1},{9,5},{13,9},{2,14},{6,2},{... | collective-permute-start | bytes 430088 | tf_op jit(solution)/shard_map/ppermute | solution.py:660
  81.9 3.6 %collective-permute-done.18.refs_1_ = bf16[56,1280]{1,0:T(8,128)(2,1)S(1)} collective-permute-done((bf16[56,1280]{1,0:T(8,128)(2,1)S(1)}, bf16[56,1280]{1,0:T(8,128)(2,1)S(1)}, u32[]{:S(2)}, u32[]{:S(2)}) %collective-permute-start.18) | collective-permute-done | bytes 143392 | tf_op jit(solution)/shard_map/ppermute | solution.py:660
  85.5 6.8 %collective-permute-done.19.refs_2_ = bf16[56,1280]{1,0:T(8,128)(2,1)S(1)} collective-permute-done((bf16[56,1280]{1,0:T(8,128)(2,1)S(1)}, bf16[56,1280]{1,0:T(8,128)(2,1)S(1)}, u32[]{:S(2)}, u32[]{:S(2)}) %collective-permute-start.19) | collective-permute-done | bytes 143392 | tf_op jit(solution)/shard_map/ppermute | solution.py:660
  94.7 4.6 %collective-permute-start.23 = (bf16[192,1280]{1,0:T(8,128)(2,1)S(1)}, bf16[192,1280]{1,0:T(8,128)(2,1)S(1)}, u32[]{:S(2)}, u32[]{:S(2)}) collective-permute-start(bf16[192,1280]{1,0:T(8,128)(2,1)S(1)} %shard_map.136.refs_0_), channel_id=1, source_target_pairs={{0,4},{4,8},{8,12},{1,5},{5,9},{9,13},{2,6},{6,10},{10,14},{3,7},{... | collective-permute-start | bytes 1474568 | tf_op jit(solution)/shard_map/ppermute | solution.py:669
  99.2 8.2 %collective-permute-done.21.refs_1_.refs_2_ = bf16[192,1280]{1,0:T(8,128)(2,1)S(1)} collective-permute-done((bf16[192,1280]{1,0:T(8,128)(2,1)S(1)}, bf16[192,1280]{1,0:T(8,128)(2,1)S(1)}, u32[]{:S(2)}, u32[]{:S(2)}) %collective-permute-start.21) | collective-permute-done | bytes 491552 | tf_op jit(solution)/shard_map/ppermute | solution.py:668
  111.2 9.9 %collective-permute-done.22 = bf16[192,1280]{1,0:T(8,128)(2,1)} collective-permute-done((bf16[192,1280]{1,0:T(8,128)(2,1)S(1)}, bf16[192,1280]{1,0:T(8,128)(2,1)}, u32[]{:S(2)}, u32[]{:S(2)}) %collective-permute-start.22) | collective-permute-done | bytes 491552 | tf_op jit(solution)/shard_map/ppermute | solution.py:674
  123.6 2.4 copy-done.6
  128.1 6.8 %shard_map.137 = (f32[2048,384]{1,0:T(8,128)S(1)}, bf16[384,1280]{1,0:T(8,128)(2,1)S(1)}, f32[2,16,192]{2,1,0:T(8,128)S(1)}) custom-call(s32[1]{0:T(128)} %bitcast.1.member_ref, bf16[2000,1280]{1,0:T(8,128)(2,1)S(1)} %bitcast.57, bf16[128,1280]{1,0:T(8,128)(2,1)S(1)} %get-tuple-element.102.label_ref, bf16[192,1280]{1,0:T(8,128)(2,1)S(1)} %shard_map.136.refs_0_, ...), custom_call_target="tpu_custom_call" | custom-call | flops 2013265920 | bytes 9437184 | tf_op jit(solution)/shard_map/pallas_call | solution.py:359
  135.7 6.6 %shard_map.138 = (f32[2048,384]{1,0:T(8,128)S(1)}, bf16[384,1280]{1,0:T(8,128)(2,1)S(1)}, f32[4,16,192]{2,1,0:T(8,128)S(1)}) custom-call(s32[1]{0:T(128)} %bitcast.1.member_ref, bf16[2000,1280]{1,0:T(8,128)(2,1)S(1)} %bitcast.58, bf16[128,1280]{1,0:T(8,128)(2,1)S(1)} %get-tuple-element.103.label_ref, bf16[192,1280]{1,0:T(8,128)(2,1)S(1)} %broadcast_select_fusion.refs_0_, ...), custom_call_target="tpu_custom_call" | custom-call | flops 2013265920 | bytes 9437184 | tf_op jit(solution)/shard_map/pallas_call | solution.py:359
  142.4 4.7 %collective-permute-start.26 = (f32[4,16,192]{2,1,0:T(8,128)S(1)}, f32[4,16,192]{2,1,0:T(8,128)S(1)}, u32[]{:S(2)}, u32[]{:S(2)}) collective-permute-start(f32[4,16,192]{2,1,0:T(8,128)S(1)} %get-tuple-element.70.refs_0_), channel_id=1, source_target_pairs={{0,12},{4,0},{8,4},{12,8},{1,13},{5,1},{9,5},{13,9},{2,14},{6,2},{... | collective-permute-start | bytes 147464 | tf_op jit(solution)/shard_map/ppermute | solution.py:660
  150.3 2.6 %collective-permute-done.27.refs_2_ = f32[4,16,192]{2,1,0:T(8,128)S(1)} collective-permute-done((f32[4,16,192]{2,1,0:T(8,128)S(1)}, f32[4,16,192]{2,1,0:T(8,128)S(1)}, u32[]{:S(2)}, u32[]{:S(2)}) %collective-permute-start.27) | collective-permute-done | bytes 49184 | tf_op jit(solution)/shard_map/ppermute | solution.py:660
  154.4 6.6 %shard_map.139 = (f32[16,768]{1,0:T(8,128)S(1)}, bf16[256,768]{1,0:T(8,128)(2,1)S(1)}, bf16[256,768]{1,0:T(8,128)(2,1)S(1)}, f32[16,128]{1,0:T(8,128)S(1)}) custom-call(s32[16]{0:T(128)S(1)} %fusion.2.slots_ref, s32[16,128]{1,0:T(8,128)S(1)} %pad.12.labels_ref, s32[16,1]{1,0:T(8,128)S(1)} %get-tuple-element.109.frames_ref, ...), custom_call_target="tpu_custom_call" | custom-call | flops 67108864 | bytes 1048576 | tf_op jit(solution)/shard_map/pallas_call | solution.py:546
  161.0 4.0 %shard_map.141 = bf16[512,1280]{1,0:T(8,128)(2,1)} custom-call(s32[2]{0:T(128)S(1)} %pad_add_fusion.4.order_ref, f32[2048,384]{1,0:T(8,128)S(1)} %get-tuple-element.72.refs_0_, f32[2048,384]{1,0:T(8,128)S(1)} %get-tuple-element.73.refs_1_, bf16[384,1280]{1,0:T(8,128)(2,1)S(1)} %get-tuple-element.74.refs_2_, bf16[384,1280]{1,0:T(8,128)(2,1)S(1)} %get-tuple-element.75.refs_3_, ...), custom_call_target="tpu_custom_call" | custom-call | flops 1409286144 | bytes 10485760 | tf_op jit(solution)/shard_map/pallas_call | solution.py:598
  170.0 2.8 %shard_map.140 = bf16[512,1280]{1,0:T(8,128)(2,1)S(1)} custom-call(s32[2]{0:T(128)S(1)} %pad_add_fusion.3.order_ref, f32[2048,384]{1,0:T(8,128)S(1)} %copy-done.2, f32[2048,384]{1,0:T(8,128)S(1)} %copy-done.4, bf16[384,1280]{1,0:T(8,128)(2,1)S(1)} %get-tuple-element.74.refs_2_, bf16[384,1280]{1,0:T(8,128)(2,1)S(1)} %get-tuple-element.75.refs_3_, ...), custom_call_target="tpu_custom_call" | custom-call | flops 1409286144 | bytes 10485760 | tf_op jit(solution)/shard_map/pallas_call | solution.py:598
  174.5 4.9 %shard_map.142 = (bf16[512,1280]{1,0:T(8,128)(2,1)}, bf16[512,1280]{1,0:T(8,128)(2,1)S(1)}) custom-call(s32[4]{0:T(128)S(1)} %pad_add_fusion.2.order_ref, f32[2048,384]{1,0:T(8,128)S(1)} %copy-done.2, f32[2048,384]{1,0:T(8,128)S(1)} %copy-done.4, bf16[384,1280]{1,0:T(8,128)(2,1)S(1)} %get-tuple-element.74.refs_2_, ...), custom_call_target="tpu_custom_call" | custom-call | flops 2818572288 | bytes 10485760 | tf_op jit(solution)/shard_map/pallas_call | solution.py:598
  185.9 12.2 %collective-permute-done.33 = bf16[256,1280]{1,0:T(8,128)(2,1)} collective-permute-done((bf16[256,1280]{1,0:T(8,128)(2,1)}, bf16[256,1280]{1,0:T(8,128)(2,1)}, u32[]{:S(2)}, u32[]{:S(2)}) %collective-permute-start.33) | collective-permute-done | bytes 655392 | tf_op jit(solution)/shard_map/ppermute | solution.py:655
  204.7 6.7 %collective-permute-done.32 = bf16[128,1280]{1,0:T(8,128)(2,1)S(1)} collective-permute-done((bf16[128,1280]{1,0:T(8,128)(2,1)S(1)}, bf16[128,1280]{1,0:T(8,128)(2,1)S(1)}, u32[]{:S(2)}, u32[]{:S(2)}) %collective-permute-start.32) | collective-permute-done | bytes 327712 | tf_op jit(solution)/shard_map/ppermute | solution.py:655
  216.5 12.1 %collective-permute-done.36 = bf16[256,1280]{1,0:T(8,128)(2,1)S(1)} collective-permute-done((bf16[256,1280]{1,0:T(8,128)(2,1)}, bf16[256,1280]{1,0:T(8,128)(2,1)S(1)}, u32[]{:S(2)}, u32[]{:S(2)}) %collective-permute-start.36) | collective-permute-done | bytes 655392 | tf_op jit(solution)/shard_map/ppermute | solution.py:655
  231.7 4.7 %collective-permute-done.37.refs_6_ = bf16[128,1280]{1,0:T(8,128)(2,1)S(1)} collective-permute-done((bf16[128,1280]{1,0:T(8,128)(2,1)S(1)}, bf16[128,1280]{1,0:T(8,128)(2,1)S(1)}, u32[]{:S(2)}, u32[]{:S(2)}) %collective-permute-start.37) | collective-permute-done | bytes 327712 | tf_op jit(solution)/shard_map/ppermute | solution.py:655
  236.4 4.0 %collective-permute-done.38.refs_7_ = bf16[128,1280]{1,0:T(8,128)(2,1)S(1)} collective-permute-done((bf16[128,1280]{1,0:T(8,128)(2,1)S(1)}, bf16[128,1280]{1,0:T(8,128)(2,1)S(1)}, u32[]{:S(2)}, u32[]{:S(2)}) %collective-permute-start.38) | collective-permute-done | bytes 327712 | tf_op jit(solution)/shard_map/ppermute | solution.py:655
  242.0 3.0 %shard_map.143 = bf16[2000,1280]{1,0:T(8,128)(2,1)} custom-call(s32[16]{0:T(128)S(1)} %stack.117.offsets_ref, bf16[128,1280]{1,0:T(8,128)(2,1)S(1)} %add_convert_fusion.5.refs_0_, bf16[128,1280]{1,0:T(8,128)(2,1)S(1)} %add_convert_fusion.4.refs_1_, bf16[128,1280]{1,0:T(8,128)(2,1)S(1)} %get-tuple-element.101.refs_2_, ...), custom_call_target="tpu_custom_call" | custom-call | bytes 10240000 | tf_op jit(solution)/shard_map/pallas_call | solution.py:643
  (211 shorter events, 81.2 us)
Async XLA Ops:
  0.7 11.5 %collective-permute-start = (s32[8,48]{1,0:T(8,128)}, s32[8,48]{1,0:T(8,128)S(1)}, u32[]{:S(2)}, u32[]{:S(2)}) collective-permute-start(s32[8,48]{1,0:T(8,128)} %bitcast.68), channel_id=1, source_target_pairs={{0,16},{16,0},{1,17},{17,1},{2,18},{18,2},{3,19},{19,3},{4,20},{20... | collective-permute-start | bytes 4616 | tf_op jit(solution)/shard_map/ppermute | solution.py:655
  6.4 27.1 %collective-permute-start.7 = (f32[16,1280]{1,0:T(8,128)}, f32[16,1280]{1,0:T(8,128)}, u32[]{:S(2)}, u32[]{:S(2)}) collective-permute-start(f32[16,1280]{1,0:T(8,128)} %maximum_maximum_fusion), channel_id=1, source_target_pairs={{0,16},{16,0},{1,17},{17,1},{2,18},{18,2},{3,19},{19,3},{4,20},{20... | collective-permute-start | bytes 245768 | tf_op jit(solution)/shard_map/ppermute | solution.py:655
  9.9 26.7 %collective-permute-start.8 = (bf16[1280,128]{1,0:T(8,128)(2,1)}, bf16[1280,128]{1,0:T(8,128)(2,1)}, u32[]{:S(2)}, u32[]{:S(2)}) collective-permute-start(bf16[1280,128]{1,0:T(8,128)(2,1)} %dynamic-slice_bitcast_fusion.1), channel_id=1, source_target_pairs={{0,16},{16,0},{1,17},{17,1},{2,18},{18,2},{3,19},{19,3},{4,20},{20... | collective-permute-start | bytes 983048 | tf_op jit(solution)/shard_map/ppermute | solution.py:655
  11.9 24.7 %collective-permute-start.9 = (bf16[128,1280]{1,0:T(8,128)(2,1)}, bf16[128,1280]{1,0:T(8,128)(2,1)}, u32[]{:S(2)}, u32[]{:S(2)}) collective-permute-start(bf16[128,1280]{1,0:T(8,128)(2,1)} %dynamic-slice_bitcast_fusion), channel_id=1, source_target_pairs={{0,16},{16,0},{1,17},{17,1},{2,18},{18,2},{3,19},{19,3},{4,20},{20... | collective-permute-start | bytes 983048 | tf_op jit(solution)/shard_map/ppermute | solution.py:655
  24.9 13.2 %collective-permute-start.4 = (bf16[56,1280]{1,0:T(8,128)(2,1)}, bf16[56,1280]{1,0:T(8,128)(2,1)}, u32[]{:S(2)}, u32[]{:S(2)}) collective-permute-start(bf16[56,1280]{1,0:T(8,128)(2,1)} %get-tuple-element.46), channel_id=1, source_target_pairs={{0,4},{4,8},{8,12},{12,0},{1,5},{5,9},{9,13},{13,1},{2,6},{6,10},{... | collective-permute-start | bytes 430088 | tf_op jit(solution)/shard_map/ppermute | solution.py:660
  25.5 12.6 %collective-permute-start.5 = (bf16[56,1280]{1,0:T(8,128)(2,1)}, bf16[56,1280]{1,0:T(8,128)(2,1)}, u32[]{:S(2)}, u32[]{:S(2)}) collective-permute-start(bf16[56,1280]{1,0:T(8,128)(2,1)} %get-tuple-element.47), channel_id=1, source_target_pairs={{0,8},{4,12},{8,0},{12,4},{1,9},{5,13},{9,1},{13,5},{2,10},{6,14},... | collective-permute-start | bytes 430088 | tf_op jit(solution)/shard_map/ppermute | solution.py:660
  45.9 10.6 %collective-permute-start.13 = (bf16[56,1280]{1,0:T(8,128)(2,1)S(1)}, bf16[56,1280]{1,0:T(8,128)(2,1)S(1)}, u32[]{:S(2)}, u32[]{:S(2)}) collective-permute-start(bf16[56,1280]{1,0:T(8,128)(2,1)S(1)} %get-tuple-element.58), channel_id=1, source_target_pairs={{0,8},{4,12},{8,0},{12,4},{1,9},{5,13},{9,1},{13,5},{2,10},{6,14},... | collective-permute-start | bytes 430088 | tf_op jit(solution)/shard_map/ppermute | solution.py:660
  46.1 10.4 %collective-permute-start.14 = (bf16[56,1280]{1,0:T(8,128)(2,1)S(1)}, bf16[56,1280]{1,0:T(8,128)(2,1)S(1)}, u32[]{:S(2)}, u32[]{:S(2)}) collective-permute-start(bf16[56,1280]{1,0:T(8,128)(2,1)S(1)} %get-tuple-element.59), channel_id=1, source_target_pairs={{0,4},{4,8},{8,12},{12,0},{1,5},{5,9},{9,13},{13,1},{2,6},{6,10},{... | collective-permute-start | bytes 430088 | tf_op jit(solution)/shard_map/ppermute | solution.py:660
  60.0 8.3 %collective-permute-start.15 = (bf16[56,1280]{1,0:T(8,128)(2,1)}, bf16[56,1280]{1,0:T(8,128)(2,1)S(1)}, u32[]{:S(2)}, u32[]{:S(2)}) collective-permute-start(bf16[56,1280]{1,0:T(8,128)(2,1)} %get-tuple-element.62), channel_id=1, source_target_pairs={{0,4},{4,8},{8,12},{12,0},{1,5},{5,9},{9,13},{13,1},{2,6},{6,10},{... | collective-permute-start | bytes 430088 | tf_op jit(solution)/shard_map/ppermute | solution.py:660
  60.0 11.2 %collective-permute-start.16 = (bf16[56,1280]{1,0:T(8,128)(2,1)}, bf16[56,1280]{1,0:T(8,128)(2,1)S(1)}, u32[]{:S(2)}, u32[]{:S(2)}) collective-permute-start(bf16[56,1280]{1,0:T(8,128)(2,1)} %get-tuple-element.63), channel_id=1, source_target_pairs={{0,8},{4,12},{8,0},{12,4},{1,9},{5,13},{9,1},{13,5},{2,10},{6,14},... | collective-permute-start | bytes 430088 | tf_op jit(solution)/shard_map/ppermute | solution.py:660
  61.2 10.0 %collective-permute-start.17 = (bf16[56,1280]{1,0:T(8,128)(2,1)}, bf16[56,1280]{1,0:T(8,128)(2,1)S(1)}, u32[]{:S(2)}, u32[]{:S(2)}) collective-permute-start(bf16[56,1280]{1,0:T(8,128)(2,1)} %get-tuple-element.64), channel_id=1, source_target_pairs={{0,12},{4,0},{8,4},{12,8},{1,13},{5,1},{9,5},{13,9},{2,14},{6,2},{... | collective-permute-start | bytes 430088 | tf_op jit(solution)/shard_map/ppermute | solution.py:660
  76.3 9.2 %collective-permute-start.18 = (bf16[56,1280]{1,0:T(8,128)(2,1)S(1)}, bf16[56,1280]{1,0:T(8,128)(2,1)S(1)}, u32[]{:S(2)}, u32[]{:S(2)}) collective-permute-start(bf16[56,1280]{1,0:T(8,128)(2,1)S(1)} %get-tuple-element.66), channel_id=1, source_target_pairs={{0,12},{4,0},{8,4},{12,8},{1,13},{5,1},{9,5},{13,9},{2,14},{6,2},{... | collective-permute-start | bytes 430088 | tf_op jit(solution)/shard_map/ppermute | solution.py:660
  81.3 11.0 %collective-permute-start.19 = (bf16[56,1280]{1,0:T(8,128)(2,1)S(1)}, bf16[56,1280]{1,0:T(8,128)(2,1)S(1)}, u32[]{:S(2)}, u32[]{:S(2)}) collective-permute-start(bf16[56,1280]{1,0:T(8,128)(2,1)S(1)} %get-tuple-element.67), channel_id=1, source_target_pairs={{0,8},{4,12},{8,0},{12,4},{1,9},{5,13},{9,1},{13,5},{2,10},{6,14},... | collective-permute-start | bytes 430088 | tf_op jit(solution)/shard_map/ppermute | solution.py:660
  81.3 11.0 %collective-permute-start.20 = (bf16[56,1280]{1,0:T(8,128)(2,1)S(1)}, bf16[56,1280]{1,0:T(8,128)(2,1)S(1)}, u32[]{:S(2)}, u32[]{:S(2)}) collective-permute-start(bf16[56,1280]{1,0:T(8,128)(2,1)S(1)} %get-tuple-element.68), channel_id=1, source_target_pairs={{0,4},{4,8},{8,12},{12,0},{1,5},{5,9},{9,13},{13,1},{2,6},{6,10},{... | collective-permute-start | bytes 430088 | tf_op jit(solution)/shard_map/ppermute | solution.py:660
  93.4 14.1 %collective-permute-start.21 = (bf16[192,1280]{1,0:T(8,128)(2,1)S(1)}, bf16[192,1280]{1,0:T(8,128)(2,1)S(1)}, u32[]{:S(2)}, u32[]{:S(2)}) collective-permute-start(bf16[192,1280]{1,0:T(8,128)(2,1)S(1)} %shard_map.136.refs_0_), channel_id=1, source_target_pairs={{4,0},{8,4},{12,8},{5,1},{9,5},{13,9},{6,2},{10,6},{14,10},{7,3},{... | collective-permute-start | bytes 1474568 | tf_op jit(solution)/shard_map/ppermute | solution.py:668
  94.7 14.1 %collective-permute-start.23 = (bf16[192,1280]{1,0:T(8,128)(2,1)S(1)}, bf16[192,1280]{1,0:T(8,128)(2,1)S(1)}, u32[]{:S(2)}, u32[]{:S(2)}) collective-permute-start(bf16[192,1280]{1,0:T(8,128)(2,1)S(1)} %shard_map.136.refs_0_), channel_id=1, source_target_pairs={{0,4},{4,8},{8,12},{1,5},{5,9},{9,13},{2,6},{6,10},{10,14},{3,7},{... | collective-permute-start | bytes 1474568 | tf_op jit(solution)/shard_map/ppermute | solution.py:669
  107.4 13.7 %collective-permute-start.22 = (bf16[192,1280]{1,0:T(8,128)(2,1)S(1)}, bf16[192,1280]{1,0:T(8,128)(2,1)}, u32[]{:S(2)}, u32[]{:S(2)}) collective-permute-start(bf16[192,1280]{1,0:T(8,128)(2,1)S(1)} %collective-permute-done.21.refs_1_.refs_2_), channel_id=1, source_target_pairs={{4,0},{8,4},{5,1},{9,5},{6,2},{10,6},{7,3},{11,7},{20,16},{24,20},... | collective-permute-start | bytes 1474568 | tf_op jit(solution)/shard_map/ppermute | solution.py:674
  108.7 12.4 %collective-permute-start.24 = (bf16[192,1280]{1,0:T(8,128)(2,1)S(1)}, bf16[192,1280]{1,0:T(8,128)(2,1)}, u32[]{:S(2)}, u32[]{:S(2)}) collective-permute-start(bf16[192,1280]{1,0:T(8,128)(2,1)S(1)} %collective-permute-done.23.refs_2_.refs_3_), channel_id=1, source_target_pairs={{4,8},{8,12},{5,9},{9,13},{6,10},{10,14},{7,11},{11,15},{20,24},{2... | collective-permute-start | bytes 1474568 | tf_op jit(solution)/shard_map/ppermute | solution.py:675
  122.2 13.5 %collective-permute-start.25 = (bf16[192,1280]{1,0:T(8,128)(2,1)S(1)}, bf16[192,1280]{1,0:T(8,128)(2,1)S(1)}, u32[]{:S(2)}, u32[]{:S(2)}) collective-permute-start(bf16[192,1280]{1,0:T(8,128)(2,1)S(1)} %broadcast_select_fusion.refs_0_), channel_id=1, source_target_pairs={{4,0},{8,12},{5,1},{9,13},{6,2},{10,14},{7,3},{11,15},{20,16},{24,... | collective-permute-start | bytes 1474568 | tf_op jit(solution)/shard_map/ppermute | solution.py:680
  142.4 8.0 %collective-permute-start.26 = (f32[4,16,192]{2,1,0:T(8,128)S(1)}, f32[4,16,192]{2,1,0:T(8,128)S(1)}, u32[]{:S(2)}, u32[]{:S(2)}) collective-permute-start(f32[4,16,192]{2,1,0:T(8,128)S(1)} %get-tuple-element.70.refs_0_), channel_id=1, source_target_pairs={{0,12},{4,0},{8,4},{12,8},{1,13},{5,1},{9,5},{13,9},{2,14},{6,2},{... | collective-permute-start | bytes 147464 | tf_op jit(solution)/shard_map/ppermute | solution.py:660
  165.0 7.8 %collective-permute-start.29 = (bf16[512,1280]{1,0:T(8,128)(2,1)}, bf16[512,1280]{1,0:T(8,128)(2,1)}, u32[]{:S(2)}, u32[]{:S(2)}) collective-permute-start(bf16[512,1280]{1,0:T(8,128)(2,1)} %shard_map.141), channel_id=1, source_target_pairs={{0,1},{1,0},{2,3},{3,2},{4,5},{5,4},{6,7},{7,6},{8,9},{9,8},{10,11... | collective-permute-start | bytes 3932168 | tf_op jit(solution)/shard_map/ppermute | solution.py:655
  180.8 17.2 %collective-permute-start.33 = (bf16[256,1280]{1,0:T(8,128)(2,1)}, bf16[256,1280]{1,0:T(8,128)(2,1)}, u32[]{:S(2)}, u32[]{:S(2)}) collective-permute-start(bf16[256,1280]{1,0:T(8,128)(2,1)} %get-tuple-element.90), channel_id=1, source_target_pairs={{0,2},{2,0},{1,3},{3,1},{4,6},{6,4},{5,7},{7,5},{8,10},{10,8},{9,1... | collective-permute-start | bytes 1966088 | tf_op jit(solution)/shard_map/ppermute | solution.py:655
  182.4 16.8 %collective-permute-start.31 = (bf16[256,1280]{1,0:T(8,128)(2,1)S(1)}, bf16[256,1280]{1,0:T(8,128)(2,1)}, u32[]{:S(2)}, u32[]{:S(2)}) collective-permute-start(bf16[256,1280]{1,0:T(8,128)(2,1)S(1)} %get-tuple-element.91), channel_id=1, source_target_pairs={{0,16},{16,0},{1,17},{17,1},{2,18},{18,2},{3,19},{19,3},{4,20},{20... | collective-permute-start | bytes 1966088 | tf_op jit(solution)/shard_map/ppermute | solution.py:655
  202.6 8.9 %collective-permute-start.32 = (bf16[128,1280]{1,0:T(8,128)(2,1)S(1)}, bf16[128,1280]{1,0:T(8,128)(2,1)S(1)}, u32[]{:S(2)}, u32[]{:S(2)}) collective-permute-start(bf16[128,1280]{1,0:T(8,128)(2,1)S(1)} %constant_dynamic-slice_fusion.1), channel_id=1, source_target_pairs={{0,2},{2,0},{1,3},{3,1},{4,6},{6,4},{5,7},{7,5},{8,10},{10,8},{9,1... | collective-permute-start | bytes 983048 | tf_op jit(solution)/shard_map/ppermute | solution.py:655
  203.1 9.3 %collective-permute-start.34 = (bf16[128,1280]{1,0:T(8,128)(2,1)S(1)}, bf16[128,1280]{1,0:T(8,128)(2,1)S(1)}, u32[]{:S(2)}, u32[]{:S(2)}) collective-permute-start(bf16[128,1280]{1,0:T(8,128)(2,1)S(1)} %constant_dynamic-slice_fusion), channel_id=1, source_target_pairs={{0,16},{16,0},{1,17},{17,1},{2,18},{18,2},{3,19},{19,3},{4,20},{20... | collective-permute-start | bytes 983048 | tf_op jit(solution)/shard_map/ppermute | solution.py:655
  213.4 15.1 %collective-permute-start.36 = (bf16[256,1280]{1,0:T(8,128)(2,1)}, bf16[256,1280]{1,0:T(8,128)(2,1)S(1)}, u32[]{:S(2)}, u32[]{:S(2)}) collective-permute-start(bf16[256,1280]{1,0:T(8,128)(2,1)} %pad_maximum_fusion), channel_id=1, source_target_pairs={{0,2},{2,0},{1,3},{3,1},{4,6},{6,4},{5,7},{7,5},{8,10},{10,8},{9,1... | collective-permute-start | bytes 1966088 | tf_op jit(solution)/shard_map/ppermute | solution.py:655
  214.3 15.9 %collective-permute-start.35 = (bf16[256,1280]{1,0:T(8,128)(2,1)}, bf16[256,1280]{1,0:T(8,128)(2,1)S(1)}, u32[]{:S(2)}, u32[]{:S(2)}) collective-permute-start(bf16[256,1280]{1,0:T(8,128)(2,1)} %pad_maximum_fusion), channel_id=1, source_target_pairs={{0,16},{16,0},{1,17},{17,1},{2,18},{18,2},{3,19},{19,3},{4,20},{20... | collective-permute-start | bytes 1966088 | tf_op jit(solution)/shard_map/ppermute | solution.py:655
  216.5 15.2 %collective-permute-start.39 = (bf16[256,1280]{1,0:T(8,128)(2,1)}, bf16[256,1280]{1,0:T(8,128)(2,1)S(1)}, u32[]{:S(2)}, u32[]{:S(2)}) collective-permute-start(bf16[256,1280]{1,0:T(8,128)(2,1)} %pad_maximum_fusion), channel_id=1, source_target_pairs={{0,1},{1,0},{2,3},{3,2},{4,5},{5,4},{6,7},{7,6},{8,9},{9,8},{10,11... | collective-permute-start | bytes 1966088 | tf_op jit(solution)/shard_map/ppermute | solution.py:655
  228.6 7.8 %collective-permute-start.37 = (bf16[128,1280]{1,0:T(8,128)(2,1)S(1)}, bf16[128,1280]{1,0:T(8,128)(2,1)S(1)}, u32[]{:S(2)}, u32[]{:S(2)}) collective-permute-start(bf16[128,1280]{1,0:T(8,128)(2,1)S(1)} %get-tuple-element.99.refs_4_), channel_id=1, source_target_pairs={{0,16},{16,0},{1,17},{17,1},{2,18},{18,2},{3,19},{19,3},{4,20},{20... | collective-permute-start | bytes 983048 | tf_op jit(solution)/shard_map/ppermute | solution.py:655
  230.2 10.2 %collective-permute-start.40 = (bf16[256,1280]{1,0:T(8,128)(2,1)S(1)}, bf16[256,1280]{1,0:T(8,128)(2,1)S(1)}, u32[]{:S(2)}, u32[]{:S(2)}) collective-permute-start(bf16[256,1280]{1,0:T(8,128)(2,1)S(1)} %collective-permute-done.35), channel_id=1, source_target_pairs={{0,1},{1,0},{2,3},{3,2},{4,5},{5,4},{6,7},{7,6},{8,9},{9,8},{10,11... | collective-permute-start | bytes 1966088 | tf_op jit(solution)/shard_map/ppermute | solution.py:655
  230.2 10.2 %collective-permute-start.38 = (bf16[128,1280]{1,0:T(8,128)(2,1)S(1)}, bf16[128,1280]{1,0:T(8,128)(2,1)S(1)}, u32[]{:S(2)}, u32[]{:S(2)}) collective-permute-start(bf16[128,1280]{1,0:T(8,128)(2,1)S(1)} %get-tuple-element.100.refs_3_), channel_id=1, source_target_pairs={{0,2},{2,0},{1,3},{3,1},{4,6},{6,4},{5,7},{7,5},{8,10},{10,8},{9,1... | collective-permute-start | bytes 983048 | tf_op jit(solution)/shard_map/ppermute | solution.py:655
  231.4 9.0 %collective-permute-start.41 = (bf16[256,1280]{1,0:T(8,128)(2,1)S(1)}, bf16[256,1280]{1,0:T(8,128)(2,1)S(1)}, u32[]{:S(2)}, u32[]{:S(2)}) collective-permute-start(bf16[256,1280]{1,0:T(8,128)(2,1)S(1)} %collective-permute-done.36), channel_id=1, source_target_pairs={{0,1},{1,0},{2,3},{3,2},{4,5},{5,4},{6,7},{7,6},{8,9},{9,8},{10,11... | collective-permute-start | bytes 1966088 | tf_op jit(solution)/shard_map/ppermute | solution.py:655
  (52 other events, 324.7 us)
where the time goes:
time: 246 us; the launch traced here: 245 us
  waiting for transfers between devices  98.9 us (40%)
  starting transfers between devices  58.2 us (24%)
  Pallas kernels  47.8 us (19%)
  local copies, waits for them, and re-layouts  26.1 us (11%)
  other arithmetic  12.7 us (5%)
    ppermute x21, waiting for transfers between devices, swap(): return lax.ppermute(value, axis, [(0, 1), (1, 0)])  42.3 us
    ppermute x18, waiting for transfers between devices, rotate(): lax.ppermute(value, axis, [(i, (i + by) % count) for i in range(count)])  37.7 us
    ppermute x18, starting transfers between devices, rotate(): lax.ppermute(value, axis, [(i, (i + by) % count) for i in range(count)])  31.7 us
    unnamed x81, local copies, waits for them, and re-layouts  18.5 us
    ppermute x21, starting transfers between devices, swap(): return lax.ppermute(value, axis, [(0, 1), (1, 0)])  16.6 us
    pallas_call x2, Pallas kernels, head_logits(): call(kernel, (jax.ShapeDtypeStruct((height, row_count), jnp.float32), bf1...  13.4 us
    pallas_call x3, Pallas kernels, head_gradient(): call(kernel, tuple((bf16_rows(each * BLOCK_ROWS, width) for _ in range(ou...  11.7 us
    ppermute x1, waiting for transfers between devices, line_far(): left = lax.ppermute(near[0], 'expert', [(1, 0), (2, 1)])  9.91 us
  transfers between devices with their start and end apart: 44, of which 21 were waited for; matrix products, arithmetic and copies ran while one was open for 6% of the time, Pallas kernels for 6%

commit v1 on v0

--- a/solution.py
+++ b/solution.py
@@ -25,20 +25,16 @@
     return pl.BlockSpec(memory_space=pltpu.VMEM)
 
 
-def hbm_spec():
-    return pl.BlockSpec(memory_space=pltpu.HBM)
-
-
 def smem_spec():
     return pl.BlockSpec(memory_space=pltpu.SMEM)
 
 
-def call(kernel, out_shape, flops=0, moved=0, **options):
+def call(kernel, out_shape, flops=0, **options):
     return pl.pallas_call(
         kernel,
         out_shape=out_shape,
         compiler_params=pltpu.CompilerParams(vmem_limit_bytes=VMEM_LIMIT),
-        cost_estimate=pl.CostEstimate(flops=flops, bytes_accessed=moved, transcendentals=0),
+        cost_estimate=pl.CostEstimate(flops=flops, bytes_accessed=0, transcendentals=0),
         **options,
     )
 
@@ -134,7 +130,6 @@
         kernel,
         tuple(bf16_rows(capacity, width) for _ in range(experts)),
         1 << 27,
-        1 << 20,
         in_specs=[smem_spec()] + [vmem_spec()] * 2,
         out_specs=tuple(vmem_spec() for _ in range(experts)),
     )(member, rows, ids)
@@ -183,7 +178,6 @@
         kernel,
         tuple(bf16_rows(capacity, width) for _ in range(count)),
         4 * count * capacity * width * own[0].shape[1],
-        4 << 20,
         in_specs=[smem_spec()] + [vmem_spec()] * (3 + 2 * others + count),
         out_specs=tuple(vmem_spec() for _ in range(count)),
     )(pick_own, table, *own, *flat, *received)
@@ -218,7 +212,6 @@
         kernel,
         shapes,
         1 << 28,
-        2 << 20,
         in_specs=[smem_spec()] + [vmem_spec()] * (4 + experts),
         out_specs=tuple(vmem_spec() for _ in shapes),
     )(member, rows, ids, table, next_ids, *returned)
@@ -245,7 +238,6 @@
         kernel,
         bf16_rows(*rows.shape),
         1 << 28,
-        2 << 20,
         in_specs=[smem_spec()] + [vmem_spec()] * (4 + experts),
         out_specs=vmem_spec(),
     )(member, rows, ids, table, head_gain, *returned)
@@ -255,30 +247,17 @@
     return [(i, min(BLOCK_ROWS, shard - i)) for i in range(0, shard, BLOCK_ROWS)]
 
 
-def weight_copies(weight_ref, held_ref, sems, shard):
-    return [
-        pltpu.make_async_copy(
-            weight_ref.at[pl.ds(first, size)], held_ref.at[pl.ds(first, size)], sems.at[index]
-        )
-        for index, (first, size) in enumerate(block_list(shard))
-    ]
-
-
 def label_rows(weight, places):
     shard, width = weight.shape
     entries = places.shape[0]
 
-    def kernel(places_ref, weight_ref, out_ref, held_ref, sems):
-        copies = weight_copies(weight_ref, held_ref, sems, shard)
-        for copy in copies:
-            copy.start()
+    def kernel(places_ref, weight_ref, out_ref):
         total = jnp.zeros((entries, width), jnp.float32)
-        for copy, (first, size) in zip(copies, block_list(shard)):
+        for first, size in block_list(shard):
             entry = first + lax.broadcasted_iota(jnp.int32, (entries, size), 1)
             chosen = as_mask(entry == places_ref[...])
-            copy.wait()
             total = total + lax.dot_general(
-                chosen, held_ref[first : first + size], NN, preferred_element_type=jnp.float32
+                chosen, weight_ref[first : first + size], NN, preferred_element_type=jnp.float32
             )
         out_ref[...] = total.astype(jnp.bfloat16)
 
@@ -286,13 +265,8 @@
         kernel,
         bf16_rows(entries, width),
         2 * shard * entries * width,
-        6 << 20,
-        in_specs=[vmem_spec(), hbm_spec()],
+        in_specs=[vmem_spec()] * 2,
         out_specs=vmem_spec(),
-        scratch_shapes=[
-            pltpu.VMEM((shard, width), jnp.bfloat16),
-            pltpu.SemaphoreType.DMA((len(block_list(shard)),)),
-        ],
     )(places, weight)
 
 
@@ -308,10 +282,7 @@
 
     def kernel(member_ref, weight_ref, label_ref, *refs):
         piece_refs = refs[:given]
-        logits_ref, rows_ref, stats_ref, held_ref, sems = refs[given + len(others) :]
-        copies = weight_copies(weight_ref, held_ref, sems, shard)
-        for copy in copies:
-            copy.start()
+        logits_ref, rows_ref, stats_ref = refs[given + len(others) :]
 
         def put(slot, piece_ref):
             rows_ref[slot * span : (slot + 1) * span] = piece_ref[...]
@@ -324,10 +295,9 @@
         fill(member_ref[0], piece_refs, put, put_if)
         peak = jnp.full((1, row_count), LOG_ZERO, jnp.float32)
         total = jnp.zeros((1, row_count), jnp.float32)
-        for copy, (first, size) in zip(copies, block_list(shard)):
-            copy.wait()
+        for first, size in block_list(shard):
             logits = lax.dot_general(
-                held_ref[first : first + size],
+                weight_ref[first : first + size],
                 rows_ref[...],
                 NT,
                 preferred_element_type=jnp.float32,
@@ -364,13 +334,8 @@
             jax.ShapeDtypeStruct((ahead + count, COLS, span), jnp.float32),
         ),
         2 * height * row_count * width,
-        9 << 20,
-        in_specs=[smem_spec(), hbm_spec()] + [vmem_spec()] * (1 + given + len(others)),
+        in_specs=[smem_spec()] + [vmem_spec()] * (2 + given + len(others)),
         out_specs=tuple(vmem_spec() for _ in range(3)),
-        scratch_shapes=[
-            pltpu.VMEM((shard, width), jnp.bfloat16),
-            pltpu.SemaphoreType.DMA((len(block_list(shard)),)),
-        ],
     )(member, weight, label_weight, *pieces, *others)
 
 
@@ -552,7 +517,6 @@
             jax.ShapeDtypeStruct((utterances, LANES), jnp.float32),
         ),
         1 << 26,
-        1 << 20,
         in_specs=[smem_spec()] + [vmem_spec()] * (3 + sources),
         out_specs=tuple(vmem_spec() for _ in range(4)),
         scratch_shapes=[pltpu.VMEM((LANES, tall), jnp.float32), table]
@@ -599,7 +563,6 @@
         kernel,
         tuple(bf16_rows(each * BLOCK_ROWS, width) for _ in range(outputs)),
         2 * blocks * BLOCK_ROWS * count * row_count * (width + 2 * entries),
-        10 << 20,
         in_specs=[smem_spec()] + [vmem_spec()] * (2 * count + 4),
         out_specs=tuple(vmem_spec() for _ in range(outputs)),
     )(order, *logits, *rows, occupancy, high, low, places)
@@ -644,7 +607,6 @@
         kernel,
         bf16_rows(height, width),
         0,
-        2 * height * width * 2,
         in_specs=[smem_spec()] + [pl.BlockSpec(memory_space=pl.ANY)] * count,
         out_specs=pl.BlockSpec(memory_space=pl.ANY),
         scratch_shapes=[pltpu.SemaphoreType.DMA((count,))],
@@ -796,7 +758,7 @@
             layers.append((all_tables[layer], chosen, [], jnp.ones((1,), jnp.int32)))
 
     labels, frame_lengths, label_lengths = lax.optimization_barrier(
-        (labels, frame_lengths, label_lengths, outgoing[0])
+        (labels, frame_lengths, label_lengths, received[1])
     )[:3]
     notes = jnp.concatenate(
         [
@@ -834,14 +796,15 @@
     ).reshape(utterances * COLS)
     local = named - member * shard
     places = jnp.where((named >= 0) & (local >= 0) & (local < shard), local, -1)
-    label_weight = label_rows(weight_rows, places.reshape(-1, 1))
-    received, label_weight = lax.optimization_barrier((received, label_weight))
     slot_entries = per_section * COLS
 
     for layer in range(sections):
         table, weights, others, pick_own = layers[layer]
         done = run_expert(received, table, weights, others, pick_own)
         returned = exchange(done, -1)
+        if layer == 0:
+            label_weight = label_rows(weight_rows, after(places.reshape(-1, 1), done[0]))
+            returned, label_weight = lax.optimization_barrier((returned, label_weight))
         if layer < sections - 1:
             current, outgoing = combine_and_dispatch(
                 current,
@@ -877,8 +840,9 @@
     if group_size == 4:
         left, right = line_near(normed)
         far = line_far((left, right), member)
+        heads = [logits_of(fill_near, 0, 2, [normed, left, right], None)]
+        far, heads[0] = lax.optimization_barrier((far, heads[0]))
         end = line_end(far)
-        heads = [logits_of(fill_near, 0, 2, [normed, left, right], None)]
         heads.append(logits_of(fill_far, 2, 2, [far, end, left, right], heads[0][2]))
         stats = heads[1][2]
         found = [stats] + [rotate(stats, "expert", -k) for k in range(1, group_size)]

time: 246 us -> 255 us (1.037)
  local copies, waits for them, and re-layouts: 26.1 us -> 40.5 us
  Pallas kernels: 47.8 us -> 38.4 us
  waiting for transfers between devices: 98.9 us -> 104 us
    ppermute x1, waiting for transfers between devices: 0.84 us -> 10.5 us  [line_end(): return lax.ppermute(far, 'expert', [(1, 0), (2, 3)])]
    unnamed x81 -> x83, local copies, waits for them, and re-layouts: 18.5 us -> 27.6 us
    ppermute x1, waiting for transfers between devices: 9.91 us -> 2.54 us  [line_far(): left = lax.ppermute(near[0], 'expert', [(1, 0), (2, 1)])]
    pallas_call x2, Pallas kernels: 13.4 us -> 6.7 us  [head_logits(): call(kernel, (jax.ShapeDtypeStruct((height, row_count), jnp.float32), bf1...]
    ppermute x18, waiting for transfers between devices: 37.7 us -> 40.5 us  [rotate(): lax.ppermute(value, axis, [(i, (i + by) % count) for i in range(count)])]
  transfers between devices with their start and end apart: 44 -> 44, of which waited for: 21 -> 21; matrix products, arithmetic and copies ran while one was open for 6% -> 8% of each run, Pallas kernels for 6% -> 4%
where the time goes in v1:
time: 255 us; the launch traced here: 254 us
  waiting for transfers between devices  104 us (41%)
  starting transfers between devices  55.7 us (22%)
  local copies, waits for them, and re-layouts  40.5 us (16%)
  Pallas kernels  38.4 us (15%)
  other arithmetic  13.7 us (5%)
    ppermute x21, waiting for transfers between devices, swap(): return lax.ppermute(value, axis, [(0, 1), (1, 0)])  42.3 us
    ppermute x18, waiting for transfers between devices, rotate(): lax.ppermute(value, axis, [(i, (i + by) % count) for i in range(count)])  40.5 us
    ppermute x18, starting transfers between devices, rotate(): lax.ppermute(value, axis, [(i, (i + by) % count) for i in range(count)])  29.9 us
    unnamed x83, local copies, waits for them, and re-layouts  27.6 us
    ppermute x21, starting transfers between devices, swap(): return lax.ppermute(value, axis, [(0, 1), (1, 0)])  16.7 us
    pallas_call x3, Pallas kernels, head_gradient(): call(kernel, tuple((bf16_rows(each * BLOCK_ROWS, width) for _ in range(ou...  11.6 us
    ppermute x1, waiting for transfers between devices, line_end(): return lax.ppermute(far, 'expert', [(1, 0), (2, 3)])  10.5 us
    ppermute x1, waiting for transfers between devices, line_near(): left = lax.ppermute(value, 'expert', [(1, 0), (2, 1), (3, 2)])  7.93 us
  transfers between devices with their start and end apart: 44, of which 21 were waited for; matrix products, arithmetic and copies ran while one was open for 8% of the time, Pallas kernels for 4%

profile of v1, /device:TPU:0, one launch (start us, length us, event | category | flops | bytes accessed | tf_op | source)
XLA Modules:
  0.0 253.5 jit_solution(4824176832228375949)
XLA Ops:
  0.7 3.0 %collective-permute-start = (s32[8,48]{1,0:T(8,128)}, s32[8,48]{1,0:T(8,128)}, u32[]{:S(2)}, u32[]{:S(2)}) collective-permute-start(s32[8,48]{1,0:T(8,128)} %bitcast.68), channel_id=1, source_target_pairs={{0,16},{16,0},{1,17},{17,1},{2,18},{18,2},{3,19},{19,3},{4,20},{20... | collective-permute-start | bytes 4616 | tf_op jit(solution)/shard_map/ppermute | solution.py:617
  17.3 2.6 %collective-permute-start.10 = (bf16[56,1280]{1,0:T(8,128)(2,1)}, bf16[56,1280]{1,0:T(8,128)(2,1)}, u32[]{:S(2)}, u32[]{:S(2)}) collective-permute-start(bf16[56,1280]{1,0:T(8,128)(2,1)} %get-tuple-element.54), channel_id=1, source_target_pairs={{0,8},{4,12},{8,0},{12,4},{1,9},{5,13},{9,1},{13,5},{2,10},{6,14},... | collective-permute-start | bytes 430088 | tf_op jit(solution)/shard_map/ppermute | solution.py:622
  30.3 3.3 %collective-permute-start.11 = (bf16[56,1280]{1,0:T(8,128)(2,1)}, bf16[56,1280]{1,0:T(8,128)(2,1)}, u32[]{:S(2)}, u32[]{:S(2)}) collective-permute-start(bf16[56,1280]{1,0:T(8,128)(2,1)} %copy-done.34), channel_id=1, source_target_pairs={{0,12},{4,0},{8,4},{12,8},{1,13},{5,1},{9,5},{13,9},{2,14},{6,2},{... | collective-permute-start | bytes 430088 | tf_op jit(solution)/shard_map/ppermute | solution.py:622
  34.1 4.0 %collective-permute-done.4 = s32[4,14]{1,0:T(4,128)S(1)} collective-permute-done((s32[4,14]{1,0:T(4,128)S(1)}, s32[4,14]{1,0:T(4,128)S(1)}, u32[]{:S(2)}, u32[]{:S(2)}) %collective-permute-start.4) | collective-permute-done | bytes 256 | tf_op jit(solution)/shard_map/ppermute | solution.py:622
  49.5 2.4 copy-done.6
  53.5 7.8 %collective-permute-done.13.refs_2_ = bf16[56,1280]{1,0:T(8,128)(2,1)S(1)} collective-permute-done((bf16[56,1280]{1,0:T(8,128)(2,1)S(1)}, bf16[56,1280]{1,0:T(8,128)(2,1)S(1)}, u32[]{:S(2)}, u32[]{:S(2)}) %collective-permute-start.13) | collective-permute-done | bytes 143392 | tf_op jit(solution)/shard_map/ppermute | solution.py:622
  67.1 2.9 %collective-permute-start.17 = (bf16[56,1280]{1,0:T(8,128)(2,1)}, bf16[56,1280]{1,0:T(8,128)(2,1)S(1)}, u32[]{:S(2)}, u32[]{:S(2)}) collective-permute-start(bf16[56,1280]{1,0:T(8,128)(2,1)} %get-tuple-element.70), channel_id=1, source_target_pairs={{0,12},{4,0},{8,4},{12,8},{1,13},{5,1},{9,5},{13,9},{2,14},{6,2},{... | collective-permute-start | bytes 430088 | tf_op jit(solution)/shard_map/ppermute | solution.py:622
  70.0 3.5 %collective-permute-done.15.refs_5_ = bf16[56,1280]{1,0:T(8,128)(2,1)S(1)} collective-permute-done((bf16[56,1280]{1,0:T(8,128)(2,1)}, bf16[56,1280]{1,0:T(8,128)(2,1)S(1)}, u32[]{:S(2)}, u32[]{:S(2)}) %collective-permute-start.15) | collective-permute-done | bytes 143392 | tf_op jit(solution)/shard_map/ppermute | solution.py:622
  73.5 4.5 %collective-permute-done.16.refs_6_ = bf16[56,1280]{1,0:T(8,128)(2,1)S(1)} collective-permute-done((bf16[56,1280]{1,0:T(8,128)(2,1)}, bf16[56,1280]{1,0:T(8,128)(2,1)S(1)}, u32[]{:S(2)}, u32[]{:S(2)}) %collective-permute-start.16) | collective-permute-done | bytes 143392 | tf_op jit(solution)/shard_map/ppermute | solution.py:622
  84.1 4.8 %collective-permute-start.18 = (bf16[56,1280]{1,0:T(8,128)(2,1)S(1)}, bf16[56,1280]{1,0:T(8,128)(2,1)S(1)}, u32[]{:S(2)}, u32[]{:S(2)}) collective-permute-start(bf16[56,1280]{1,0:T(8,128)(2,1)S(1)} %get-tuple-element.72), channel_id=1, source_target_pairs={{0,12},{4,0},{8,4},{12,8},{1,13},{5,1},{9,5},{13,9},{2,14},{6,2},{... | collective-permute-start | bytes 430088 | tf_op jit(solution)/shard_map/ppermute | solution.py:622
  89.5 3.6 %collective-permute-done.18.refs_1_ = bf16[56,1280]{1,0:T(8,128)(2,1)S(1)} collective-permute-done((bf16[56,1280]{1,0:T(8,128)(2,1)S(1)}, bf16[56,1280]{1,0:T(8,128)(2,1)S(1)}, u32[]{:S(2)}, u32[]{:S(2)}) %collective-permute-start.18) | collective-permute-done | bytes 143392 | tf_op jit(solution)/shard_map/ppermute | solution.py:622
  93.1 8.1 %collective-permute-done.19.refs_2_ = bf16[56,1280]{1,0:T(8,128)(2,1)S(1)} collective-permute-done((bf16[56,1280]{1,0:T(8,128)(2,1)S(1)}, bf16[56,1280]{1,0:T(8,128)(2,1)S(1)}, u32[]{:S(2)}, u32[]{:S(2)}) %collective-permute-start.19) | collective-permute-done | bytes 143392 | tf_op jit(solution)/shard_map/ppermute | solution.py:622
  103.4 4.6 %collective-permute-start.23 = (bf16[192,1280]{1,0:T(8,128)(2,1)S(1)}, bf16[192,1280]{1,0:T(8,128)(2,1)S(1)}, u32[]{:S(2)}, u32[]{:S(2)}) collective-permute-start(bf16[192,1280]{1,0:T(8,128)(2,1)S(1)} %shard_map.136.refs_0_), channel_id=1, source_target_pairs={{0,4},{4,8},{8,12},{1,5},{5,9},{9,13},{2,6},{6,10},{10,14},{3,7},{... | collective-permute-start | bytes 1474568 | tf_op jit(solution)/shard_map/ppermute | solution.py:631
  108.0 7.9 %collective-permute-done.21.refs_1_.refs_2_ = bf16[192,1280]{1,0:T(8,128)(2,1)S(1)} collective-permute-done((bf16[192,1280]{1,0:T(8,128)(2,1)S(1)}, bf16[192,1280]{1,0:T(8,128)(2,1)S(1)}, u32[]{:S(2)}, u32[]{:S(2)}) %collective-permute-start.21) | collective-permute-done | bytes 491552 | tf_op jit(solution)/shard_map/ppermute | solution.py:630
  118.7 2.4 copy-done.7
  121.2 3.4 %shard_map.137 = (f32[2048,384]{1,0:T(8,128)S(1)}, bf16[384,1280]{1,0:T(8,128)(2,1)S(1)}, f32[2,16,192]{2,1,0:T(8,128)S(1)}) custom-call(s32[1]{0:T(128)} %bitcast.1.member_ref, bf16[2000,1280]{1,0:T(8,128)(2,1)S(1)} %bitcast.57, bf16[128,1280]{1,0:T(8,128)(2,1)S(1)} %get-tuple-element.112.label_ref, bf16[192,1280]{1,0:T(8,128)(2,1)S(1)} %shard_map.136.refs_0_, ...), custom_call_target="tpu_custom_call" | custom-call | flops 2013265920 | tf_op jit(solution)/shard_map/pallas_call | solution.py:329
  126.3 2.5 %collective-permute-done.22 = bf16[192,1280]{1,0:T(8,128)(2,1)S(1)} collective-permute-done((bf16[192,1280]{1,0:T(8,128)(2,1)S(1)}, bf16[192,1280]{1,0:T(8,128)(2,1)S(1)}, u32[]{:S(2)}, u32[]{:S(2)}) %collective-permute-start.22) | collective-permute-done | bytes 491552 | tf_op jit(solution)/shard_map/ppermute | solution.py:636
  131.2 10.5 %collective-permute-done.25.refs_1_ = bf16[192,1280]{1,0:T(8,128)(2,1)S(1)} collective-permute-done((bf16[192,1280]{1,0:T(8,128)(2,1)S(1)}, bf16[192,1280]{1,0:T(8,128)(2,1)S(1)}, u32[]{:S(2)}, u32[]{:S(2)}) %collective-permute-start.25) | collective-permute-done | bytes 491552 | tf_op jit(solution)/shard_map/ppermute | solution.py:642
  142.5 2.4 copy-done.8
  149.1 3.3 %shard_map.138 = (f32[2048,384]{1,0:T(8,128)S(1)}, bf16[384,1280]{1,0:T(8,128)(2,1)S(1)}, f32[4,16,192]{2,1,0:T(8,128)S(1)}) custom-call(s32[1]{0:T(128)} %bitcast.1.member_ref, bf16[2000,1280]{1,0:T(8,128)(2,1)S(1)} %bitcast.58, bf16[128,1280]{1,0:T(8,128)(2,1)S(1)} %copy-done.21, bf16[192,1280]{1,0:T(8,128)(2,1)S(1)} %broadcast_select_fusion.refs_0_, ...), custom_call_target="tpu_custom_call" | custom-call | flops 2013265920 | tf_op jit(solution)/shard_map/pallas_call | solution.py:329
  152.3 4.4 %collective-permute-start.26 = (f32[4,16,192]{2,1,0:T(8,128)S(1)}, f32[4,16,192]{2,1,0:T(8,128)S(1)}, u32[]{:S(2)}, u32[]{:S(2)}) collective-permute-start(f32[4,16,192]{2,1,0:T(8,128)S(1)} %get-tuple-element.80.refs_0_), channel_id=1, source_target_pairs={{0,12},{4,0},{8,4},{12,8},{1,13},{5,1},{9,5},{13,9},{2,14},{6,2},{... | collective-permute-start | bytes 147464 | tf_op jit(solution)/shard_map/ppermute | solution.py:622
  158.6 3.3 %collective-permute-done.27.refs_2_ = f32[4,16,192]{2,1,0:T(8,128)S(1)} collective-permute-done((f32[4,16,192]{2,1,0:T(8,128)S(1)}, f32[4,16,192]{2,1,0:T(8,128)S(1)}, u32[]{:S(2)}, u32[]{:S(2)}) %collective-permute-start.27) | collective-permute-done | bytes 49184 | tf_op jit(solution)/shard_map/ppermute | solution.py:622
  162.8 6.6 %shard_map.139 = (f32[16,768]{1,0:T(8,128)S(1)}, bf16[256,768]{1,0:T(8,128)(2,1)S(1)}, bf16[256,768]{1,0:T(8,128)(2,1)S(1)}, f32[16,128]{1,0:T(8,128)S(1)}) custom-call(s32[16]{0:T(128)S(1)} %fusion.2.slots_ref, s32[16,128]{1,0:T(8,128)S(1)} %pad.12.labels_ref, s32[16,1]{1,0:T(8,128)S(1)} %get-tuple-element.119.frames_ref, ...), custom_call_target="tpu_custom_call" | custom-call | flops 67108864 | tf_op jit(solution)/shard_map/pallas_call | solution.py:511
  169.4 3.9 %shard_map.141 = bf16[512,1280]{1,0:T(8,128)(2,1)} custom-call(s32[2]{0:T(128)S(1)} %pad_add_fusion.4.order_ref, f32[2048,384]{1,0:T(8,128)S(1)} %copy-done.2, f32[2048,384]{1,0:T(8,128)S(1)} %get-tuple-element.83.refs_1_, bf16[384,1280]{1,0:T(8,128)(2,1)S(1)} %get-tuple-element.84.refs_2_, bf16[384,1280]{1,0:T(8,128)(2,1)S(1)} %get-tuple-element.85.refs_3_, ...), custom_call_target="tpu_custom_call" | custom-call | flops 1409286144 | tf_op jit(solution)/shard_map/pallas_call | solution.py:562
  178.3 2.8 %shard_map.140 = bf16[512,1280]{1,0:T(8,128)(2,1)S(1)} custom-call(s32[2]{0:T(128)S(1)} %pad_add_fusion.3.order_ref, f32[2048,384]{1,0:T(8,128)S(1)} %copy-done.3, f32[2048,384]{1,0:T(8,128)S(1)} %copy-done.5, bf16[384,1280]{1,0:T(8,128)(2,1)S(1)} %get-tuple-element.84.refs_2_, bf16[384,1280]{1,0:T(8,128)(2,1)S(1)} %get-tuple-element.85.refs_3_, ...), custom_call_target="tpu_custom_call" | custom-call | flops 1409286144 | tf_op jit(solution)/shard_map/pallas_call | solution.py:562
  182.8 4.9 %shard_map.142 = (bf16[512,1280]{1,0:T(8,128)(2,1)}, bf16[512,1280]{1,0:T(8,128)(2,1)S(1)}) custom-call(s32[4]{0:T(128)S(1)} %pad_add_fusion.2.order_ref, f32[2048,384]{1,0:T(8,128)S(1)} %copy-done.3, f32[2048,384]{1,0:T(8,128)S(1)} %copy-done.5, bf16[384,1280]{1,0:T(8,128)(2,1)S(1)} %get-tuple-element.84.refs_2_, ...), custom_call_target="tpu_custom_call" | custom-call | flops 2818572288 | tf_op jit(solution)/shard_map/pallas_call | solution.py:562
  194.2 12.2 %collective-permute-done.33 = bf16[256,1280]{1,0:T(8,128)(2,1)} collective-permute-done((bf16[256,1280]{1,0:T(8,128)(2,1)}, bf16[256,1280]{1,0:T(8,128)(2,1)}, u32[]{:S(2)}, u32[]{:S(2)}) %collective-permute-start.33) | collective-permute-done | bytes 655392 | tf_op jit(solution)/shard_map/ppermute | solution.py:617
  213.1 6.7 %collective-permute-done.32 = bf16[128,1280]{1,0:T(8,128)(2,1)S(1)} collective-permute-done((bf16[128,1280]{1,0:T(8,128)(2,1)S(1)}, bf16[128,1280]{1,0:T(8,128)(2,1)S(1)}, u32[]{:S(2)}, u32[]{:S(2)}) %collective-permute-start.32) | collective-permute-done | bytes 327712 | tf_op jit(solution)/shard_map/ppermute | solution.py:617
  224.8 12.1 %collective-permute-done.36 = bf16[256,1280]{1,0:T(8,128)(2,1)S(1)} collective-permute-done((bf16[256,1280]{1,0:T(8,128)(2,1)}, bf16[256,1280]{1,0:T(8,128)(2,1)S(1)}, u32[]{:S(2)}, u32[]{:S(2)}) %collective-permute-start.36) | collective-permute-done | bytes 655392 | tf_op jit(solution)/shard_map/ppermute | solution.py:617
  240.0 4.8 %collective-permute-done.37.refs_6_ = bf16[128,1280]{1,0:T(8,128)(2,1)S(1)} collective-permute-done((bf16[128,1280]{1,0:T(8,128)(2,1)S(1)}, bf16[128,1280]{1,0:T(8,128)(2,1)S(1)}, u32[]{:S(2)}, u32[]{:S(2)}) %collective-permute-start.37) | collective-permute-done | bytes 327712 | tf_op jit(solution)/shard_map/ppermute | solution.py:617
  244.8 4.0 %collective-permute-done.38.refs_7_ = bf16[128,1280]{1,0:T(8,128)(2,1)S(1)} collective-permute-done((bf16[128,1280]{1,0:T(8,128)(2,1)S(1)}, bf16[128,1280]{1,0:T(8,128)(2,1)S(1)}, u32[]{:S(2)}, u32[]{:S(2)}) %collective-permute-start.38) | collective-permute-done | bytes 327712 | tf_op jit(solution)/shard_map/ppermute | solution.py:617
  250.4 3.0 %shard_map.143 = bf16[2000,1280]{1,0:T(8,128)(2,1)} custom-call(s32[16]{0:T(128)S(1)} %stack.117.offsets_ref, bf16[128,1280]{1,0:T(8,128)(2,1)S(1)} %add_convert_fusion.5.refs_0_, bf16[128,1280]{1,0:T(8,128)(2,1)S(1)} %add_convert_fusion.4.refs_1_, bf16[128,1280]{1,0:T(8,128)(2,1)S(1)} %get-tuple-element.111.refs_2_, ...), custom_call_target="tpu_custom_call" | custom-call | tf_op jit(solution)/shard_map/pallas_call | solution.py:606
  (213 shorter events, 95.9 us)
Async XLA Ops:
  0.7 11.8 %collective-permute-start = (s32[8,48]{1,0:T(8,128)}, s32[8,48]{1,0:T(8,128)}, u32[]{:S(2)}, u32[]{:S(2)}) collective-permute-start(s32[8,48]{1,0:T(8,128)} %bitcast.68), channel_id=1, source_target_pairs={{0,16},{16,0},{1,17},{17,1},{2,18},{18,2},{3,19},{19,3},{4,20},{20... | collective-permute-start | bytes 4616 | tf_op jit(solution)/shard_map/ppermute | solution.py:617
  5.3 14.6 %collective-permute-start.5 = (f32[16,1280]{1,0:T(8,128)S(1)}, f32[16,1280]{1,0:T(8,128)}, u32[]{:S(2)}, u32[]{:S(2)}) collective-permute-start(f32[16,1280]{1,0:T(8,128)S(1)} %maximum_maximum_fusion), channel_id=1, source_target_pairs={{0,16},{16,0},{1,17},{17,1},{2,18},{18,2},{3,19},{19,3},{4,20},{20... | collective-permute-start | bytes 245768 | tf_op jit(solution)/shard_map/ppermute | solution.py:617
  9.0 29.1 %collective-permute-start.6 = (bf16[1280,128]{1,0:T(8,128)(2,1)}, bf16[1280,128]{1,0:T(8,128)(2,1)S(1)}, u32[]{:S(2)}, u32[]{:S(2)}) collective-permute-start(bf16[1280,128]{1,0:T(8,128)(2,1)} %dynamic-slice_bitcast_fusion.1), channel_id=1, source_target_pairs={{0,16},{16,0},{1,17},{17,1},{2,18},{18,2},{3,19},{19,3},{4,20},{20... | collective-permute-start | bytes 983048 | tf_op jit(solution)/shard_map/ppermute | solution.py:617
  11.0 27.2 %collective-permute-start.7 = (bf16[128,1280]{1,0:T(8,128)(2,1)}, bf16[128,1280]{1,0:T(8,128)(2,1)S(1)}, u32[]{:S(2)}, u32[]{:S(2)}) collective-permute-start(bf16[128,1280]{1,0:T(8,128)(2,1)} %dynamic-slice_bitcast_fusion), channel_id=1, source_target_pairs={{0,16},{16,0},{1,17},{17,1},{2,18},{18,2},{3,19},{19,3},{4,20},{20... | collective-permute-start | bytes 983048 | tf_op jit(solution)/shard_map/ppermute | solution.py:617
  15.3 8.3 %collective-permute-start.1 = (bf16[56,1280]{1,0:T(8,128)(2,1)S(1)}, bf16[56,1280]{1,0:T(8,128)(2,1)S(1)}, u32[]{:S(2)}, u32[]{:S(2)}) collective-permute-start(bf16[56,1280]{1,0:T(8,128)(2,1)S(1)} %get-tuple-element.47), channel_id=1, source_target_pairs={{0,4},{4,8},{8,12},{12,0},{1,5},{5,9},{9,13},{13,1},{2,6},{6,10},{... | collective-permute-start | bytes 430088 | tf_op jit(solution)/shard_map/ppermute | solution.py:622
  17.3 24.2 %collective-permute-start.10 = (bf16[56,1280]{1,0:T(8,128)(2,1)}, bf16[56,1280]{1,0:T(8,128)(2,1)}, u32[]{:S(2)}, u32[]{:S(2)}) collective-permute-start(bf16[56,1280]{1,0:T(8,128)(2,1)} %get-tuple-element.54), channel_id=1, source_target_pairs={{0,8},{4,12},{8,0},{12,4},{1,9},{5,13},{9,1},{13,5},{2,10},{6,14},... | collective-permute-start | bytes 430088 | tf_op jit(solution)/shard_map/ppermute | solution.py:622
  30.3 11.2 %collective-permute-start.11 = (bf16[56,1280]{1,0:T(8,128)(2,1)}, bf16[56,1280]{1,0:T(8,128)(2,1)}, u32[]{:S(2)}, u32[]{:S(2)}) collective-permute-start(bf16[56,1280]{1,0:T(8,128)(2,1)} %copy-done.34), channel_id=1, source_target_pairs={{0,12},{4,0},{8,4},{12,8},{1,13},{5,1},{9,5},{13,9},{2,14},{6,2},{... | collective-permute-start | bytes 430088 | tf_op jit(solution)/shard_map/ppermute | solution.py:622
  45.5 7.9 %collective-permute-start.12 = (bf16[56,1280]{1,0:T(8,128)(2,1)S(1)}, bf16[56,1280]{1,0:T(8,128)(2,1)S(1)}, u32[]{:S(2)}, u32[]{:S(2)}) collective-permute-start(bf16[56,1280]{1,0:T(8,128)(2,1)S(1)} %get-tuple-element.57), channel_id=1, source_target_pairs={{0,12},{4,0},{8,4},{12,8},{1,13},{5,1},{9,5},{13,9},{2,14},{6,2},{... | collective-permute-start | bytes 430088 | tf_op jit(solution)/shard_map/ppermute | solution.py:622
  47.9 13.4 %collective-permute-start.13 = (bf16[56,1280]{1,0:T(8,128)(2,1)S(1)}, bf16[56,1280]{1,0:T(8,128)(2,1)S(1)}, u32[]{:S(2)}, u32[]{:S(2)}) collective-permute-start(bf16[56,1280]{1,0:T(8,128)(2,1)S(1)} %get-tuple-element.58), channel_id=1, source_target_pairs={{0,8},{4,12},{8,0},{12,4},{1,9},{5,13},{9,1},{13,5},{2,10},{6,14},... | collective-permute-start | bytes 430088 | tf_op jit(solution)/shard_map/ppermute | solution.py:622
  48.3 13.0 %collective-permute-start.14 = (bf16[56,1280]{1,0:T(8,128)(2,1)S(1)}, bf16[56,1280]{1,0:T(8,128)(2,1)S(1)}, u32[]{:S(2)}, u32[]{:S(2)}) collective-permute-start(bf16[56,1280]{1,0:T(8,128)(2,1)S(1)} %get-tuple-element.59), channel_id=1, source_target_pairs={{0,4},{4,8},{8,12},{12,0},{1,5},{5,9},{9,13},{13,1},{2,6},{6,10},{... | collective-permute-start | bytes 430088 | tf_op jit(solution)/shard_map/ppermute | solution.py:622
  64.8 8.7 %collective-permute-start.15 = (bf16[56,1280]{1,0:T(8,128)(2,1)}, bf16[56,1280]{1,0:T(8,128)(2,1)S(1)}, u32[]{:S(2)}, u32[]{:S(2)}) collective-permute-start(bf16[56,1280]{1,0:T(8,128)(2,1)} %get-tuple-element.68), channel_id=1, source_target_pairs={{0,4},{4,8},{8,12},{12,0},{1,5},{5,9},{9,13},{13,1},{2,6},{6,10},{... | collective-permute-start | bytes 430088 | tf_op jit(solution)/shard_map/ppermute | solution.py:622
  65.2 12.9 %collective-permute-start.16 = (bf16[56,1280]{1,0:T(8,128)(2,1)}, bf16[56,1280]{1,0:T(8,128)(2,1)S(1)}, u32[]{:S(2)}, u32[]{:S(2)}) collective-permute-start(bf16[56,1280]{1,0:T(8,128)(2,1)} %get-tuple-element.69), channel_id=1, source_target_pairs={{0,8},{4,12},{8,0},{12,4},{1,9},{5,13},{9,1},{13,5},{2,10},{6,14},... | collective-permute-start | bytes 430088 | tf_op jit(solution)/shard_map/ppermute | solution.py:622
  67.1 11.0 %collective-permute-start.17 = (bf16[56,1280]{1,0:T(8,128)(2,1)}, bf16[56,1280]{1,0:T(8,128)(2,1)S(1)}, u32[]{:S(2)}, u32[]{:S(2)}) collective-permute-start(bf16[56,1280]{1,0:T(8,128)(2,1)} %get-tuple-element.70), channel_id=1, source_target_pairs={{0,12},{4,0},{8,4},{12,8},{1,13},{5,1},{9,5},{13,9},{2,14},{6,2},{... | collective-permute-start | bytes 430088 | tf_op jit(solution)/shard_map/ppermute | solution.py:622
  84.1 9.0 %collective-permute-start.18 = (bf16[56,1280]{1,0:T(8,128)(2,1)S(1)}, bf16[56,1280]{1,0:T(8,128)(2,1)S(1)}, u32[]{:S(2)}, u32[]{:S(2)}) collective-permute-start(bf16[56,1280]{1,0:T(8,128)(2,1)S(1)} %get-tuple-element.72), channel_id=1, source_target_pairs={{0,12},{4,0},{8,4},{12,8},{1,13},{5,1},{9,5},{13,9},{2,14},{6,2},{... | collective-permute-start | bytes 430088 | tf_op jit(solution)/shard_map/ppermute | solution.py:622
  88.8 12.3 %collective-permute-start.19 = (bf16[56,1280]{1,0:T(8,128)(2,1)S(1)}, bf16[56,1280]{1,0:T(8,128)(2,1)S(1)}, u32[]{:S(2)}, u32[]{:S(2)}) collective-permute-start(bf16[56,1280]{1,0:T(8,128)(2,1)S(1)} %get-tuple-element.73), channel_id=1, source_target_pairs={{0,8},{4,12},{8,0},{12,4},{1,9},{5,13},{9,1},{13,5},{2,10},{6,14},... | collective-permute-start | bytes 430088 | tf_op jit(solution)/shard_map/ppermute | solution.py:622
  88.8 12.3 %collective-permute-start.20 = (bf16[56,1280]{1,0:T(8,128)(2,1)S(1)}, bf16[56,1280]{1,0:T(8,128)(2,1)S(1)}, u32[]{:S(2)}, u32[]{:S(2)}) collective-permute-start(bf16[56,1280]{1,0:T(8,128)(2,1)S(1)} %get-tuple-element.74), channel_id=1, source_target_pairs={{0,4},{4,8},{8,12},{12,0},{1,5},{5,9},{9,13},{13,1},{2,6},{6,10},{... | collective-permute-start | bytes 430088 | tf_op jit(solution)/shard_map/ppermute | solution.py:622
  102.1 13.8 %collective-permute-start.21 = (bf16[192,1280]{1,0:T(8,128)(2,1)S(1)}, bf16[192,1280]{1,0:T(8,128)(2,1)S(1)}, u32[]{:S(2)}, u32[]{:S(2)}) collective-permute-start(bf16[192,1280]{1,0:T(8,128)(2,1)S(1)} %shard_map.136.refs_0_), channel_id=1, source_target_pairs={{4,0},{8,4},{12,8},{5,1},{9,5},{13,9},{6,2},{10,6},{14,10},{7,3},{... | collective-permute-start | bytes 1474568 | tf_op jit(solution)/shard_map/ppermute | solution.py:630
  103.4 13.8 %collective-permute-start.23 = (bf16[192,1280]{1,0:T(8,128)(2,1)S(1)}, bf16[192,1280]{1,0:T(8,128)(2,1)S(1)}, u32[]{:S(2)}, u32[]{:S(2)}) collective-permute-start(bf16[192,1280]{1,0:T(8,128)(2,1)S(1)} %shard_map.136.refs_0_), channel_id=1, source_target_pairs={{0,4},{4,8},{8,12},{1,5},{5,9},{9,13},{2,6},{6,10},{10,14},{3,7},{... | collective-permute-start | bytes 1474568 | tf_op jit(solution)/shard_map/ppermute | solution.py:631
  116.0 12.9 %collective-permute-start.22 = (bf16[192,1280]{1,0:T(8,128)(2,1)S(1)}, bf16[192,1280]{1,0:T(8,128)(2,1)S(1)}, u32[]{:S(2)}, u32[]{:S(2)}) collective-permute-start(bf16[192,1280]{1,0:T(8,128)(2,1)S(1)} %collective-permute-done.21.refs_1_.refs_2_), channel_id=1, source_target_pairs={{4,0},{8,4},{5,1},{9,5},{6,2},{10,6},{7,3},{11,7},{20,16},{24,20},... | collective-permute-start | bytes 1474568 | tf_op jit(solution)/shard_map/ppermute | solution.py:636
  117.3 11.6 %collective-permute-start.24 = (bf16[192,1280]{1,0:T(8,128)(2,1)S(1)}, bf16[192,1280]{1,0:T(8,128)(2,1)S(1)}, u32[]{:S(2)}, u32[]{:S(2)}) collective-permute-start(bf16[192,1280]{1,0:T(8,128)(2,1)S(1)} %collective-permute-done.23.refs_2_.refs_3_), channel_id=1, source_target_pairs={{4,8},{8,12},{5,9},{9,13},{6,10},{10,14},{7,11},{11,15},{20,24},{2... | collective-permute-start | bytes 1474568 | tf_op jit(solution)/shard_map/ppermute | solution.py:637
  128.9 12.8 %collective-permute-start.25 = (bf16[192,1280]{1,0:T(8,128)(2,1)S(1)}, bf16[192,1280]{1,0:T(8,128)(2,1)S(1)}, u32[]{:S(2)}, u32[]{:S(2)}) collective-permute-start(bf16[192,1280]{1,0:T(8,128)(2,1)S(1)} %broadcast_select_fusion.refs_0_), channel_id=1, source_target_pairs={{4,0},{8,12},{5,1},{9,13},{6,2},{10,14},{7,3},{11,15},{20,16},{24,... | collective-permute-start | bytes 1474568 | tf_op jit(solution)/shard_map/ppermute | solution.py:642
  189.2 17.2 %collective-permute-start.33 = (bf16[256,1280]{1,0:T(8,128)(2,1)}, bf16[256,1280]{1,0:T(8,128)(2,1)}, u32[]{:S(2)}, u32[]{:S(2)}) collective-permute-start(bf16[256,1280]{1,0:T(8,128)(2,1)} %get-tuple-element.100), channel_id=1, source_target_pairs={{0,2},{2,0},{1,3},{3,1},{4,6},{6,4},{5,7},{7,5},{8,10},{10,8},{9,1... | collective-permute-start | bytes 1966088 | tf_op jit(solution)/shard_map/ppermute | solution.py:617
  190.7 16.8 %collective-permute-start.31 = (bf16[256,1280]{1,0:T(8,128)(2,1)S(1)}, bf16[256,1280]{1,0:T(8,128)(2,1)}, u32[]{:S(2)}, u32[]{:S(2)}) collective-permute-start(bf16[256,1280]{1,0:T(8,128)(2,1)S(1)} %get-tuple-element.101), channel_id=1, source_target_pairs={{0,16},{16,0},{1,17},{17,1},{2,18},{18,2},{3,19},{19,3},{4,20},{20... | collective-permute-start | bytes 1966088 | tf_op jit(solution)/shard_map/ppermute | solution.py:617
  210.9 8.9 %collective-permute-start.32 = (bf16[128,1280]{1,0:T(8,128)(2,1)S(1)}, bf16[128,1280]{1,0:T(8,128)(2,1)S(1)}, u32[]{:S(2)}, u32[]{:S(2)}) collective-permute-start(bf16[128,1280]{1,0:T(8,128)(2,1)S(1)} %constant_dynamic-slice_fusion.1), channel_id=1, source_target_pairs={{0,2},{2,0},{1,3},{3,1},{4,6},{6,4},{5,7},{7,5},{8,10},{10,8},{9,1... | collective-permute-start | bytes 983048 | tf_op jit(solution)/shard_map/ppermute | solution.py:617
  211.5 9.3 %collective-permute-start.34 = (bf16[128,1280]{1,0:T(8,128)(2,1)S(1)}, bf16[128,1280]{1,0:T(8,128)(2,1)S(1)}, u32[]{:S(2)}, u32[]{:S(2)}) collective-permute-start(bf16[128,1280]{1,0:T(8,128)(2,1)S(1)} %constant_dynamic-slice_fusion), channel_id=1, source_target_pairs={{0,16},{16,0},{1,17},{17,1},{2,18},{18,2},{3,19},{19,3},{4,20},{20... | collective-permute-start | bytes 983048 | tf_op jit(solution)/shard_map/ppermute | solution.py:617
  221.8 15.1 %collective-permute-start.36 = (bf16[256,1280]{1,0:T(8,128)(2,1)}, bf16[256,1280]{1,0:T(8,128)(2,1)S(1)}, u32[]{:S(2)}, u32[]{:S(2)}) collective-permute-start(bf16[256,1280]{1,0:T(8,128)(2,1)} %pad_maximum_fusion), channel_id=1, source_target_pairs={{0,2},{2,0},{1,3},{3,1},{4,6},{6,4},{5,7},{7,5},{8,10},{10,8},{9,1... | collective-permute-start | bytes 1966088 | tf_op jit(solution)/shard_map/ppermute | solution.py:617
  222.6 15.9 %collective-permute-start.35 = (bf16[256,1280]{1,0:T(8,128)(2,1)}, bf16[256,1280]{1,0:T(8,128)(2,1)S(1)}, u32[]{:S(2)}, u32[]{:S(2)}) collective-permute-start(bf16[256,1280]{1,0:T(8,128)(2,1)} %pad_maximum_fusion), channel_id=1, source_target_pairs={{0,16},{16,0},{1,17},{17,1},{2,18},{18,2},{3,19},{19,3},{4,20},{20... | collective-permute-start | bytes 1966088 | tf_op jit(solution)/shard_map/ppermute | solution.py:617
  224.8 15.2 %collective-permute-start.39 = (bf16[256,1280]{1,0:T(8,128)(2,1)}, bf16[256,1280]{1,0:T(8,128)(2,1)S(1)}, u32[]{:S(2)}, u32[]{:S(2)}) collective-permute-start(bf16[256,1280]{1,0:T(8,128)(2,1)} %pad_maximum_fusion), channel_id=1, source_target_pairs={{0,1},{1,0},{2,3},{3,2},{4,5},{5,4},{6,7},{7,6},{8,9},{9,8},{10,11... | collective-permute-start | bytes 1966088 | tf_op jit(solution)/shard_map/ppermute | solution.py:617
  237.0 7.8 %collective-permute-start.37 = (bf16[128,1280]{1,0:T(8,128)(2,1)S(1)}, bf16[128,1280]{1,0:T(8,128)(2,1)S(1)}, u32[]{:S(2)}, u32[]{:S(2)}) collective-permute-start(bf16[128,1280]{1,0:T(8,128)(2,1)S(1)} %get-tuple-element.109.refs_4_), channel_id=1, source_target_pairs={{0,16},{16,0},{1,17},{17,1},{2,18},{18,2},{3,19},{19,3},{4,20},{20... | collective-permute-start | bytes 983048 | tf_op jit(solution)/shard_map/ppermute | solution.py:617
  238.5 10.2 %collective-permute-start.40 = (bf16[256,1280]{1,0:T(8,128)(2,1)S(1)}, bf16[256,1280]{1,0:T(8,128)(2,1)S(1)}, u32[]{:S(2)}, u32[]{:S(2)}) collective-permute-start(bf16[256,1280]{1,0:T(8,128)(2,1)S(1)} %collective-permute-done.35), channel_id=1, source_target_pairs={{0,1},{1,0},{2,3},{3,2},{4,5},{5,4},{6,7},{7,6},{8,9},{9,8},{10,11... | collective-permute-start | bytes 1966088 | tf_op jit(solution)/shard_map/ppermute | solution.py:617
  238.6 10.2 %collective-permute-start.38 = (bf16[128,1280]{1,0:T(8,128)(2,1)S(1)}, bf16[128,1280]{1,0:T(8,128)(2,1)S(1)}, u32[]{:S(2)}, u32[]{:S(2)}) collective-permute-start(bf16[128,1280]{1,0:T(8,128)(2,1)S(1)} %get-tuple-element.110.refs_3_), channel_id=1, source_target_pairs={{0,2},{2,0},{1,3},{3,1},{4,6},{6,4},{5,7},{7,5},{8,10},{10,8},{9,1... | collective-permute-start | bytes 983048 | tf_op jit(solution)/shard_map/ppermute | solution.py:617
  239.8 9.0 %collective-permute-start.41 = (bf16[256,1280]{1,0:T(8,128)(2,1)S(1)}, bf16[256,1280]{1,0:T(8,128)(2,1)S(1)}, u32[]{:S(2)}, u32[]{:S(2)}) collective-permute-start(bf16[256,1280]{1,0:T(8,128)(2,1)S(1)} %collective-permute-done.36), channel_id=1, source_target_pairs={{0,1},{1,0},{2,3},{3,2},{4,5},{5,4},{6,7},{7,6},{8,9},{9,8},{10,11... | collective-permute-start | bytes 1966088 | tf_op jit(solution)/shard_map/ppermute | solution.py:617
  (53 other events, 310.9 us)

commit v2 on v1

--- a/solution.py
+++ b/solution.py
@@ -135,20 +135,25 @@
     )(member, rows, ids)
 
 
-def run_expert(received, table, own, other, pick_own):
+def pick_table(pick_ref, tables):
+    if len(tables) == 1:
+        return tables[0][...]
+    return jnp.where(pick_ref[0] == 1, tables[0][...], tables[1][...])
+
+
+def run_expert(received, tables, own, other, pick_own):
     count = len(received)
     capacity, width = received[0].shape
-    others = len(other)
-
-    def kernel(pick_ref, table_ref, in_ref, out_weight_ref, *refs):
-        other_refs, received_refs, out_refs = (
-            refs[: 2 * others],
-            refs[2 * others : 2 * others + count],
-            refs[2 * others + count :],
-        )
+    others, choices = len(other), len(tables)
+
+    def kernel(pick_ref, in_ref, out_weight_ref, *refs):
+        table_refs, refs = refs[:choices], refs[choices:]
+        other_refs, refs = refs[: 2 * others], refs[2 * others :]
+        received_refs, out_refs = refs[:count], refs[count:]
 
         def work(pieces):
-            normed = rms_scale(join_rows(received_refs), table_ref[:1])
+            gain = pick_table(pick_ref, table_refs)[:1]
+            normed = rms_scale(join_rows(received_refs), gain)
             total = None
             for weight_in, weight_out in pieces:
                 hidden = lax.dot_general(
@@ -178,23 +183,25 @@
         kernel,
         tuple(bf16_rows(capacity, width) for _ in range(count)),
         4 * count * capacity * width * own[0].shape[1],
-        in_specs=[smem_spec()] + [vmem_spec()] * (3 + 2 * others + count),
+        in_specs=[smem_spec()] + [vmem_spec()] * (2 + choices + 2 * others + count),
         out_specs=tuple(vmem_spec() for _ in range(count)),
-    )(pick_own, table, *own, *flat, *received)
+    )(pick_own, *own, *tables, *flat, *received)
 
 
 def combine_and_dispatch(
-    rows, returned, ids, table, next_ids, member, experts, capacity, frame_count
+    rows, returned, ids, tables, pick_own, next_ids, member, experts, capacity, frame_count
 ):
     width = rows.shape[1]
-
-    def kernel(member_ref, rows_ref, ids_ref, table_ref, next_ref, *refs):
+    choices = len(tables)
+
+    def kernel(member_ref, pick_ref, rows_ref, ids_ref, next_ref, *refs):
+        table_refs, refs = refs[:choices], refs[choices:]
         returned_refs, x_ref, out_refs = refs[:experts], refs[experts], refs[experts + 1 :]
         mixed = combine_rows(
             rows_ref[...],
             returned_refs,
             ids_ref[...],
-            table_ref[...],
+            pick_table(pick_ref, table_refs),
             member_ref[0],
             experts,
             capacity,
@@ -212,21 +219,24 @@
         kernel,
         shapes,
         1 << 28,
-        in_specs=[smem_spec()] + [vmem_spec()] * (4 + experts),
+        in_specs=[smem_spec()] * 2 + [vmem_spec()] * (3 + choices + experts),
         out_specs=tuple(vmem_spec() for _ in shapes),
-    )(member, rows, ids, table, next_ids, *returned)
+    )(member, pick_own, rows, ids, next_ids, *tables, *returned)
     return result[0], result[1:]
 
 
 def combine_and_norm(
-    rows, returned, ids, table, head_gain, member, experts, capacity, frame_count
+    rows, returned, ids, tables, pick_own, head_gain, member, experts, capacity, frame_count
 ):
-    def kernel(member_ref, rows_ref, ids_ref, table_ref, head_ref, *refs):
+    choices = len(tables)
+
+    def kernel(member_ref, pick_ref, rows_ref, ids_ref, head_ref, *refs):
+        table_refs, refs = refs[:choices], refs[choices:]
         final = combine_rows(
             rows_ref[...],
             refs[:experts],
             ids_ref[...],
-            table_ref[...],
+            pick_table(pick_ref, table_refs),
             member_ref[0],
             experts,
             capacity,
@@ -238,46 +248,92 @@
         kernel,
         bf16_rows(*rows.shape),
         1 << 28,
-        in_specs=[smem_spec()] + [vmem_spec()] * (4 + experts),
+        in_specs=[smem_spec()] * 2 + [vmem_spec()] * (3 + choices + experts),
         out_specs=vmem_spec(),
-    )(member, rows, ids, table, head_gain, *returned)
+    )(member, pick_own, rows, ids, head_gain, *tables, *returned)
 
 
 def block_list(shard):
     return [(i, min(BLOCK_ROWS, shard - i)) for i in range(0, shard, BLOCK_ROWS)]
 
 
-def label_rows(weight, places):
+def label_rows(weight, notes, member, label_max, line):
     shard, width = weight.shape
-    entries = places.shape[0]
-
-    def kernel(places_ref, weight_ref, out_ref):
+    sources = len(notes)
+    pairs, columns = notes[0].shape
+    utterances = sources * pairs
+    entries = utterances * COLS
+
+    def kernel(member_ref, weight_ref, *refs):
+        note_refs = refs[:sources]
+        out_ref, places_ref, names_ref, turned_ref = refs[sources:]
+        place = member_ref[0]
+        found = [ref[...] for ref in note_refs]
+        if line:
+            low = place < 2
+            found = [
+                found[0],
+                jnp.where(low, found[1], found[3]),
+                found[2],
+                jnp.where(low, found[3], found[1]),
+            ]
+        names_ref[...] = jnp.zeros(names_ref.shape, jnp.int32)
+        for slot in range(sources):
+            names_ref[slot * pairs : (slot + 1) * pairs, :columns] = found[slot]
+        lane = lax.broadcasted_iota(jnp.int32, (utterances, LANES), 1)
+        named = jnp.where(lane < label_max, names_ref[...], jnp.where(lane == label_max, 0, -1))
+        local = named - place * shard
+        local = jnp.where((named >= 0) & (local >= 0) & (local < shard), local, -1)
+        square = jnp.concatenate(
+            [
+                local.astype(jnp.float32),
+                jnp.full((LANES - utterances, LANES), -1.0, jnp.float32),
+            ],
+            axis=0,
+        )
+        turned = jnp.transpose(square, (1, 0))
+        for utterance in range(utterances):
+            turned_ref[utterance * COLS : (utterance + 1) * COLS] = jnp.broadcast_to(
+                turned[:COLS, utterance : utterance + 1], (COLS, LANES)
+            )
+        places = turned_ref[:, :1].astype(jnp.int32)
+        places_ref[...] = jnp.transpose(turned_ref[...], (1, 0))[:1].astype(jnp.int32)
         total = jnp.zeros((entries, width), jnp.float32)
         for first, size in block_list(shard):
             entry = first + lax.broadcasted_iota(jnp.int32, (entries, size), 1)
-            chosen = as_mask(entry == places_ref[...])
             total = total + lax.dot_general(
-                chosen, weight_ref[first : first + size], NN, preferred_element_type=jnp.float32
+                as_mask(entry == places),
+                weight_ref[first : first + size],
+                NN,
+                preferred_element_type=jnp.float32,
             )
         out_ref[...] = total.astype(jnp.bfloat16)
 
     return call(
         kernel,
-        bf16_rows(entries, width),
+        (
+            bf16_rows(entries, width),
+            jax.ShapeDtypeStruct((1, entries), jnp.int32),
+            jax.ShapeDtypeStruct((utterances, LANES), jnp.int32),
+        ),
         2 * shard * entries * width,
-        in_specs=[vmem_spec()] * 2,
-        out_specs=vmem_spec(),
-    )(places, weight)
-
-
-def head_logits(fill, count, pieces, member, weight, label_weight, frame_count, earlier):
+        in_specs=[smem_spec()] + [vmem_spec()] * (1 + sources),
+        out_specs=tuple(vmem_spec() for _ in range(3)),
+        scratch_shapes=[pltpu.VMEM((entries, LANES), jnp.float32)],
+    )(member, weight, *notes)
+
+
+def head_logits(
+    fill, first_slot, count, pieces, member, weight, label_weight, frame_count, earlier
+):
     given = len(pieces)
     ahead = 0 if earlier is None else earlier.shape[0]
     span, width = pieces[0].shape
     row_count = count * span
     shard = weight.shape[0]
     height = round_up(shard, BLOCK_ROWS)
-    entries = label_weight.shape[0]
+    entries = row_count // frame_count * COLS
+    first_entry = first_slot * entries // count
     others = [] if earlier is None else [earlier]
 
     def kernel(member_ref, weight_ref, label_ref, *refs):
@@ -311,7 +367,10 @@
         if height > shard:
             logits_ref[shard:] = jnp.full((height - shard, row_count), LOG_ZERO, jnp.float32)
         crossed = lax.dot_general(
-            label_ref[...], rows_ref[...], NT, preferred_element_type=jnp.float32
+            label_ref[first_entry : first_entry + entries],
+            rows_ref[...],
+            NT,
+            preferred_element_type=jnp.float32,
         )
         owner = lax.broadcasted_iota(jnp.int32, (COLS, row_count), 1) // frame_count
         picked = jnp.zeros((COLS, row_count), jnp.float32)
@@ -347,9 +406,11 @@
 
 
 def fill_far(place, piece_refs, put, put_if):
-    far_ref, end_ref, left_ref, right_ref = piece_refs
-    put(0, far_ref)
-    put_if((place == 0) | (place == 3), 1, end_ref)
+    left_far, right_far, left_end, right_end, left_ref, right_ref = piece_refs
+    put_if(place < 2, 0, left_far)
+    put_if(place >= 2, 0, right_far)
+    put_if(place == 0, 1, left_end)
+    put_if(place == 3, 1, right_end)
     put_if(place == 1, 1, right_ref)
     put_if(place == 2, 1, left_ref)
 
@@ -371,15 +432,15 @@
     )
 
 
-def ctc_pass(stats, slots, labels, frame_counts, label_counts, frame_count, label_max):
+def ctc_pass(stats, slots, notes, frame_count, label_max, kept):
     sources = len(stats)
     count, _, span = stats[0].shape
     row_count = count * span
-    utterances = labels.shape[0]
+    utterances = notes.shape[0]
     entries = utterances * COLS
     tall = round_up(span, LANES)
 
-    def kernel(slots_ref, labels_ref, frames_ref, counts_ref, *refs):
+    def kernel(slots_ref, notes_ref, *refs):
         (
             out_ref,
             high_ref,
@@ -416,13 +477,13 @@
         lane = lax.broadcasted_iota(jnp.int32, (utterances, LANES), 1)
         is_label = lane < label_max
         is_blank = lane <= label_max
-        names = labels_ref[...]
+        names = jnp.where(is_label, notes_ref[...], 0)
         earlier = pltpu.roll(names, 1, 1)
         skip = is_label & (lane >= 1) & (names != 0) & (names != earlier)
         later = pltpu.roll(names, LANES - 1, 1)
         skip_next = (lane < label_max - 1) & (later != 0) & (later != names)
-        frames = frames_ref[...]
-        counts = counts_ref[...]
+        frames = notes_ref[:, label_max : label_max + 1]
+        counts = notes_ref[:, label_max + 1 : label_max + 2]
         ends_blank = jnp.where(lane == counts, 0.0, LOG_ZERO)
         ends_label = jnp.where(lane == counts - 1, 0.0, LOG_ZERO)
 
@@ -475,7 +536,7 @@
         end_state = jnp.sum(jnp.where(lane == counts, fwd_blank, 0.0), axis=1, keepdims=True)
         near_state = jnp.sum(jnp.where(lane == counts - 1, fwd_label, 0.0), axis=1, keepdims=True)
         log_like = log_add(end_state, near_state)
-        loss_ref[...] = jnp.broadcast_to(-log_like, (utterances, LANES))
+        loss_ref[...] = -log_like[:kept]
 
         def occupy(step, carry):
             blank = jnp.exp(blank_fwd[step] + blank_bwd[step] - log_like)
@@ -514,15 +575,15 @@
             jax.ShapeDtypeStruct((COLS, row_count), jnp.float32),
             bf16_rows(entries, row_count),
             bf16_rows(entries, row_count),
-            jax.ShapeDtypeStruct((utterances, LANES), jnp.float32),
+            jax.ShapeDtypeStruct((kept, 1), jnp.float32),
         ),
         1 << 26,
-        in_specs=[smem_spec()] + [vmem_spec()] * (3 + sources),
+        in_specs=[smem_spec()] + [vmem_spec()] * (1 + sources),
         out_specs=tuple(vmem_spec() for _ in range(4)),
         scratch_shapes=[pltpu.VMEM((LANES, tall), jnp.float32), table]
         + [held] * 6
         + [table],
-    )(slots, labels, frame_counts, label_counts, *stats)
+    )(slots, notes, *stats)
 
 
 def head_gradient(logits, rows, occupancy, high, low, places, order, outputs, each):
@@ -632,14 +693,18 @@
     return left, right
 
 
-def line_far(near, member):
-    left = lax.ppermute(near[0], "expert", [(1, 0), (2, 1)])
-    right = lax.ppermute(near[1], "expert", [(1, 2), (2, 3)])
-    return jnp.where(member < 2, left, right)
-
-
-def line_end(far):
-    return lax.ppermute(far, "expert", [(1, 0), (2, 3)])
+def line_far(left, right):
+    return (
+        lax.ppermute(left, "expert", [(1, 0), (2, 1)]),
+        lax.ppermute(right, "expert", [(1, 2), (2, 3)]),
+    )
+
+
+def line_end(left_far, right_far):
+    return (
+        lax.ppermute(left_far, "expert", [(1, 0)]),
+        lax.ppermute(right_far, "expert", [(2, 3)]),
+    )
 
 
 LINE_ORDER = np.array([[0, 1, 2, 3], [1, 2, 3, 0], [2, 1, 0, 3], [3, 2, 1, 0]])
@@ -660,8 +725,60 @@
     return tables.reshape(count, count * count)
 
 
-def add(first, second):
-    return (first.astype(jnp.float32) + second.astype(jnp.float32)).astype(jnp.bfloat16)
+def wide(ref, start, size):
+    return ref[pl.ds(start, size), :].astype(jnp.float32)
+
+
+def sum_sent(own, came, places):
+    height, width = own.shape
+    part = height // 4
+
+    def kernel(places_ref, own_ref, came_ref, *out_refs):
+        section, outer = places_ref[0], places_ref[1]
+        starts = (
+            (1 - outer) * part,
+            outer * part,
+            (2 + 1 - section) * part,
+            (2 + section) * part,
+        )
+        for start, out_ref in zip(starts, out_refs):
+            start = pl.multiple_of(start, part)
+            out_ref[...] = (wide(own_ref, start, part) + wide(came_ref, start, part)).astype(
+                jnp.bfloat16
+            )
+
+    return call(
+        kernel,
+        tuple(bf16_rows(part, width) for _ in range(4)),
+        1 << 20,
+        in_specs=[smem_spec()] + [vmem_spec()] * 2,
+        out_specs=tuple(vmem_spec() for _ in range(4)),
+    )(places, own, came)
+
+
+def sum_kept(own, came, arrived, places, keep):
+    height, width = own.shape
+    part = height // 4
+    count = len(arrived) // 2
+
+    def kernel(places_ref, own_ref, came_ref, *refs):
+        section, outer = places_ref[0], places_ref[1]
+        if not keep:
+            section, outer = 1 - section, 1 - outer
+        for side, start in enumerate((outer * part, (2 + section) * part)):
+            start = pl.multiple_of(start, part)
+            total = wide(own_ref, start, part) + wide(came_ref, start, part)
+            for ref in refs[side * count : (side + 1) * count]:
+                total = total + ref[...].astype(jnp.float32)
+            refs[2 * count + side][...] = total.astype(jnp.bfloat16)
+
+    return call(
+        kernel,
+        (bf16_rows(part, width), bf16_rows(part, width)),
+        1 << 20,
+        in_specs=[smem_spec()] + [vmem_spec()] * (2 + 2 * count),
+        out_specs=(vmem_spec(), vmem_spec()),
+    )(places, own, came, *arrived)
 
 
 def per_device(
@@ -720,9 +837,6 @@
     else:
         all_ids = lax.all_gather(own_ids, "section")
     layer_ids = [lanes_of(all_ids[layer]) for layer in range(sections)]
-    outgoing = dispatch(current, layer_ids[0], member_ref, experts, capacity, frame_count)
-    received = exchange(outgoing, 1)
-
     own_table = jnp.concatenate(
         [
             norm_gain,
@@ -733,6 +847,7 @@
         axis=0,
     )
     own = (w_in[0, 0], w_out[0, 0])
+    layers = []
     if paired:
         other_table = swap(own_table, "section")
         half = hidden // 2
@@ -742,23 +857,22 @@
         came_in = swap(sent_in, "section")
         came_out = swap(sent_out, "section")
         other = [(came_in, came_out), (swap(came_in, "dpi"), swap(came_out, "dpi"))]
+        for layer in range(sections):
+            mine = (section_id == layer).astype(jnp.int32).reshape(1)
+            layers.append(((own_table, other_table), own, other, mine))
     else:
         all_tables = lax.all_gather(own_table, "section")
         all_in = lax.all_gather(own[0], "section")
         all_out = lax.all_gather(own[1], "section")
-
-    layers = []
-    for layer in range(sections):
-        if paired:
-            mine = section_id == layer
-            table = jnp.where(mine, own_table, other_table)
-            layers.append((table, own, other, mine.astype(jnp.int32).reshape(1)))
-        else:
+        for layer in range(sections):
             chosen = (all_in[layer], all_out[layer])
-            layers.append((all_tables[layer], chosen, [], jnp.ones((1,), jnp.int32)))
+            layers.append(((all_tables[layer],), chosen, [], jnp.ones((1,), jnp.int32)))
+
+    outgoing = dispatch(current, layer_ids[0], member_ref, experts, capacity, frame_count)
+    received = exchange(outgoing, 1)
 
     labels, frame_lengths, label_lengths = lax.optimization_barrier(
-        (labels, frame_lengths, label_lengths, received[1])
+        (labels, frame_lengths, label_lengths, outgoing[0])
     )[:3]
     notes = jnp.concatenate(
         [
@@ -768,49 +882,74 @@
         ],
         axis=1,
     )
-    if group_size == 4:
-        found = [notes] + [rotate(notes, "expert", -k) for k in range(1, group_size)]
-        low = member < 2
-        notes_all = jnp.stack(
-            [
-                found[0],
-                jnp.where(low, found[1], found[3]),
-                found[2],
-                jnp.where(low, found[3], found[1]),
-            ]
-        )
-    else:
-        notes_all = lax.all_gather(notes, "expert")
     shard = head_weight.shape[1]
     weight_rows = jnp.transpose(head_weight)
-    notes_all = notes_all.reshape(-1, label_max + 2)
-    utterances = notes_all.shape[0]
-    names = notes_all[:, :label_max]
-    named = jnp.concatenate(
-        [
-            names,
-            jnp.zeros((utterances, 1), jnp.int32),
-            jnp.full((utterances, COLS - label_max - 1), -1, jnp.int32),
-        ],
-        axis=1,
-    ).reshape(utterances * COLS)
-    local = named - member * shard
-    places = jnp.where((named >= 0) & (local >= 0) & (local < shard), local, -1)
-    slot_entries = per_section * COLS
+    line = group_size == 4
+    tables = jnp.asarray(slot_tables(group_size))
+    slots = lax.dynamic_index_in_dim(tables, member, 0, keepdims=False)
+    outer = lax.axis_index("dpo")
+    blocks = -(-shard // BLOCK_ROWS)
+    tree = paired and outer_size == 2 and blocks == 8
+
+    def pair_of(side, first, second):
+        return [side * 4 + first, side * 4 + 2 + second]
+
+    def offset_of(side, s, y):
+        base = side * 4 * BLOCK_ROWS
+        part = BLOCK_ROWS // 2
+        return [
+            base + s * BLOCK_ROWS + y * part,
+            base + 2 * BLOCK_ROWS + y * BLOCK_ROWS + s * part,
+        ]
+
+    def whole_numbers(values):
+        return jnp.stack([jnp.asarray(value, jnp.int32) for value in values])
+
+    here, there = (section_id, outer), (1 - section_id, 1 - outer)
+    sibling_sent_order = whole_numbers(pair_of(1 - core, *there))
+    own_sent_order = whole_numbers(pair_of(core, *there))
+    kept_order = whole_numbers(pair_of(1 - core, *here) + pair_of(core, *here))
+    chip_place = whole_numbers(here)
+    offsets = []
+    for side in (core, 1 - core):
+        for s in (section_id, 1 - section_id):
+            for y in (outer, 1 - outer):
+                offsets += offset_of(side, s, y)
+    offsets = whole_numbers(offsets)
+    early = (
+        notes,
+        slots,
+        head_gain.reshape(1, width),
+        layer_ids[1:],
+        sibling_sent_order,
+        own_sent_order,
+        kept_order,
+        chip_place,
+        offsets,
+    )
+    early, received = lax.optimization_barrier((early, received))
+    notes, slots, head_row, later_ids, sibling_sent_order, own_sent_order = early[:6]
+    kept_order, chip_place, offsets = early[6:]
+    layer_ids = [layer_ids[0]] + list(later_ids)
 
     for layer in range(sections):
-        table, weights, others, pick_own = layers[layer]
-        done = run_expert(received, table, weights, others, pick_own)
+        choices, weights, others, pick_own = layers[layer]
+        done = run_expert(received, choices, weights, others, pick_own)
         returned = exchange(done, -1)
         if layer == 0:
-            label_weight = label_rows(weight_rows, after(places.reshape(-1, 1), done[0]))
-            returned, label_weight = lax.optimization_barrier((returned, label_weight))
+            notes = after(notes, done[0])
+            if line:
+                found = [notes] + [rotate(notes, "expert", -k) for k in range(1, group_size)]
+            else:
+                gathered = lax.all_gather(notes, "expert")
+                found = [gathered[k] for k in range(group_size)]
         if layer < sections - 1:
             current, outgoing = combine_and_dispatch(
                 current,
                 returned,
                 layer_ids[layer],
-                table,
+                choices,
+                pick_own,
                 layer_ids[layer + 1],
                 member_ref,
                 experts,
@@ -818,13 +957,20 @@
                 frame_count,
             )
             received = exchange(outgoing, 1)
+            if layer == 0:
+                found[0] = after(found[0], current)
+                label_weight, places, names = label_rows(
+                    weight_rows, found, member_ref, label_max, line
+                )
+                received, label_weight = lax.optimization_barrier((received, label_weight))
         else:
             normed = combine_and_norm(
                 current,
                 returned,
                 layer_ids[layer],
-                table,
-                head_gain.reshape(1, width),
+                choices,
+                pick_own,
+                head_row,
                 member_ref,
                 experts,
                 capacity,
@@ -832,18 +978,17 @@
             )
 
     def logits_of(fill, first, count, pieces, earlier):
-        chosen = label_weight[first * slot_entries : (first + count) * slot_entries]
         return head_logits(
-            fill, count, pieces, member_ref, weight_rows, chosen, frame_count, earlier
-        )
-
-    if group_size == 4:
+            fill, first, count, pieces, member_ref, weight_rows, label_weight, frame_count, earlier
+        )
+
+    if line:
         left, right = line_near(normed)
-        far = line_far((left, right), member)
+        far = line_far(left, right)
         heads = [logits_of(fill_near, 0, 2, [normed, left, right], None)]
         far, heads[0] = lax.optimization_barrier((far, heads[0]))
-        end = line_end(far)
-        heads.append(logits_of(fill_far, 2, 2, [far, end, left, right], heads[0][2]))
+        end = line_end(*far)
+        heads.append(logits_of(fill_far, 2, 2, [*far, *end, left, right], heads[0][2]))
         stats = heads[1][2]
         found = [stats] + [rotate(stats, "expert", -k) for k in range(1, group_size)]
     else:
@@ -855,19 +1000,12 @@
             lax.dynamic_index_in_dim(gathered, (member + k) % group_size, 0, keepdims=False)
             for k in range(group_size)
         ]
-    tables = jnp.asarray(slot_tables(group_size))
-    slots = lax.dynamic_index_in_dim(tables, member, 0, keepdims=False)
+    kept_losses = per_section if line else group_size * per_section
     occupancy, high, low, losses = ctc_pass(
-        found,
-        slots,
-        jnp.pad(names, ((0, 0), (0, LANES - label_max))),
-        notes_all[:, label_max : label_max + 1],
-        notes_all[:, label_max + 1 :],
-        frame_count,
-        label_max,
-    )
-    own_slot = 0 if group_size == 4 else member
-    my_losses = lax.dynamic_slice(losses, (own_slot * per_section, 0), (per_section, 1))
+        found, slots, names, frame_count, label_max, kept_losses
+    )
+    if not line:
+        losses = lax.dynamic_slice(losses, (member * per_section, 0), (per_section, 1))
 
     def gradient(order, outputs, each):
         return head_gradient(
@@ -876,75 +1014,34 @@
             occupancy,
             high,
             low,
-            places.reshape(1, -1),
+            places,
             order,
             outputs,
             each,
         )
 
-    blocks = heads[0][0].shape[0] // BLOCK_ROWS
-    if paired and outer_size == 2 and blocks == 8:
-        outer = lax.axis_index("dpo")
-
-        def pair_of(side, first, second):
-            return jnp.stack([side * 4 + first, side * 4 + 2 + second]).astype(jnp.int32)
-
-        came_sent = swap(
-            gradient(pair_of(1 - core, 1 - section_id, 1 - outer), 1, 2)[0], "dpi"
-        )
-        sent = add(gradient(pair_of(core, 1 - section_id, 1 - outer), 1, 2)[0], came_sent)
-        first_in = swap(sent[:BLOCK_ROWS], "section")
-        second_in = swap(sent[BLOCK_ROWS:], "dpo")
-        order = jnp.concatenate(
-            [pair_of(1 - core, section_id, outer), pair_of(core, section_id, outer)]
-        )
-        sibling_kept, own_kept = gradient(after(order, sent), 2, 2)
-        kept = add(own_kept, swap(sibling_kept, "dpi"))
-        first = add(kept[:BLOCK_ROWS], first_in)
-        second = add(kept[BLOCK_ROWS:], second_in)
-        part = BLOCK_ROWS // 2
-
-        def piece(value, index):
-            return lax.dynamic_slice_in_dim(value, index * part, part, 0)
-
-        first_far = swap(piece(first, 1 - outer), "dpo")
-        second_far = swap(piece(second, 1 - section_id), "section")
-        final = jnp.concatenate(
-            [add(piece(first, outer), first_far), add(piece(second, section_id), second_far)],
-            axis=0,
-        )
-        across = swap(final, "section")
-        beside = swap(final, "dpo")
-        first_diagonal = swap(beside[:part], "section")
-        second_diagonal = swap(across[part:], "dpo")
-        mine = [final, across, beside, first_diagonal, second_diagonal]
-        theirs = [swap(value, "dpi") for value in mine]
-        pieces, offsets = [], []
-        for side, held in ((core, mine), (1 - core, theirs)):
-            where = (
-                (section_id, outer),
-                (1 - section_id, outer),
-                (section_id, 1 - outer),
-            )
-            for value, (s, y) in zip(held[:3], where):
-                pieces += [value[:part], value[part:]]
-                offsets += [
-                    side * 1024 + s * 256 + y * 128,
-                    side * 1024 + 512 + y * 256 + s * 128,
-                ]
-            pieces += held[3:]
-            s, y = 1 - section_id, 1 - outer
-            offsets += [
-                side * 1024 + s * 256 + y * 128,
-                side * 1024 + 512 + y * 256 + s * 128,
-            ]
-        whole = assemble(pieces, jnp.stack(offsets).astype(jnp.int32), shard)
+    if tree:
+        came_sent = swap(gradient(sibling_sent_order, 1, 2)[0], "dpi")
+        own_sent = gradient(own_sent_order, 1, 2)[0]
+        a_far, a_near, b_far, b_near = sum_sent(own_sent, came_sent, chip_place)
+        a_far, b_far = swap(a_far, "section"), swap(b_far, "dpo")
+        a_near, b_near = swap(a_near, "section"), swap(b_near, "dpo")
+        sibling_kept, own_kept = gradient(after(kept_order, own_sent), 2, 2)
+        came_kept = swap(sibling_kept, "dpi")
+        a_on, b_on = sum_kept(own_kept, came_kept, [a_far, b_far], chip_place, False)
+        a_in, b_in = swap(a_on, "dpo"), swap(b_on, "section")
+        a, b = sum_kept(own_kept, came_kept, [a_near, a_in, b_near, b_in], chip_place, True)
+        a_y, b_x = swap(a, "dpo"), swap(b, "section")
+        b_y, a_x = swap(b, "dpo"), swap(a, "section")
+        a_xy, b_xy = swap(a_y, "section"), swap(b_x, "dpo")
+        mine = [a, b, a_y, b_y, a_x, b_x, a_xy, b_xy]
+        whole = assemble(mine + [swap(value, "dpi") for value in mine], offsets, shard)
     else:
         partial = gradient(jnp.arange(blocks, dtype=jnp.int32), 1, blocks)[0][:shard]
         whole = lax.psum(partial.astype(jnp.float32), ("section", "dpo", "dpi")).astype(
             jnp.bfloat16
         )
-    return (my_losses, jnp.transpose(whole))
+    return (losses, jnp.transpose(whole))
 
 
 def solution(mesh):

time: 255 us -> 288 us (1.13)
  Pallas kernels: 38.4 us -> 104 us
  local copies, waits for them, and re-layouts: 40.5 us -> 16.6 us
  other arithmetic: 13.7 us -> 0.39 us
  starting transfers between devices: 55.7 us -> 64.9 us
  waiting for transfers between devices: 104 us -> 97.3 us
    pallas_call x1, Pallas kernels: 2.96 us -> 67.6 us  [assemble(): call(kernel, bf16_rows(height, width), 0, in_specs=[smem_spec()] + [pl.Bl...]
    unnamed x83 -> x51, local copies, waits for them, and re-layouts: 27.6 us -> 11.7 us
    convert_element_type x5 -> x0, other arithmetic: 7.25 us -> none  [add(): (first.astype(jnp.float32) + second.astype(jnp.float32)).astype(jnp.bfloa...]
    ppermute x18, waiting for transfers between devices: 40.5 us -> 34 us  [rotate(): lax.ppermute(value, axis, [(i, (i + by) % count) for i in range(count)])]
    ppermute x21 -> x28, starting transfers between devices: 16.7 us -> 21.7 us  [swap(): return lax.ppermute(value, axis, [(0, 1), (1, 0)])]
    ppermute x3 -> x4, waiting for transfers between devices: 13 us -> 16.6 us  [the longest x1 10.9 us: line_end(): lax.ppermute(left_far, 'expert', [(1, 0)])]
    ppermute x18, starting transfers between devices: 29.9 us -> 33.4 us  [rotate(): lax.ppermute(value, axis, [(i, (i + by) % count) for i in range(count)])]
    pallas_call x3 -> x6, Pallas kernels: 4.63 us -> 7.38 us  [the longest x1 2.1 us: combine_and_dispatch(): call(kernel, shapes, 1 << 28, in_specs=[smem_spec()] * 2 + [vmem_spec()]...]
  transfers between devices with their start and end apart: 44 -> 52, of which waited for: 21 -> 29; matrix products, arithmetic and copies ran while one was open for 8% -> 2% of each run, Pallas kernels for 4% -> 5%
where the time goes in v2:
time: 288 us; the launch traced here: 285 us
  Pallas kernels  104 us (36%)
  waiting for transfers between devices  97.3 us (34%)
  starting transfers between devices  64.9 us (23%)
  local copies, waits for them, and re-layouts  16.6 us (6%)
    pallas_call x1, Pallas kernels, assemble(): call(kernel, bf16_rows(height, width), 0, in_specs=[smem_spec()] + [pl.Bl...  67.6 us
    ppermute x28, waiting for transfers between devices, swap(): return lax.ppermute(value, axis, [(0, 1), (1, 0)])  39.6 us
    ppermute x18, waiting for transfers between devices, rotate(): lax.ppermute(value, axis, [(i, (i + by) % count) for i in range(count)])  34 us
    ppermute x18, starting transfers between devices, rotate(): lax.ppermute(value, axis, [(i, (i + by) % count) for i in range(count)])  33.4 us
    ppermute x28, starting transfers between devices, swap(): return lax.ppermute(value, axis, [(0, 1), (1, 0)])  21.7 us
    unnamed x51, local copies, waits for them, and re-layouts  11.7 us
    ppermute x1, waiting for transfers between devices, line_end(): lax.ppermute(left_far, 'expert', [(1, 0)])  10.9 us
    pallas_call x3, Pallas kernels, head_gradient(): call(kernel, tuple((bf16_rows(each * BLOCK_ROWS, width) for _ in range(ou...  10.6 us
  transfers between devices with their start and end apart: 52, of which 29 were waited for; matrix products, arithmetic and copies ran while one was open for 2% of the time, Pallas kernels for 5%

profile of v2, /device:TPU:0, one launch (start us, length us, event | category | flops | bytes accessed | tf_op | source)
XLA Modules:
  0.0 284.6 jit_solution(1322315805484152653)
XLA Ops:
  0.7 3.0 %collective-permute-start = (s32[8,48]{1,0:T(8,128)}, s32[8,48]{1,0:T(8,128)S(1)}, u32[]{:S(2)}, u32[]{:S(2)}) collective-permute-start(s32[8,48]{1,0:T(8,128)} %bitcast.56), channel_id=1, source_target_pairs={{0,16},{16,0},{1,17},{17,1},{2,18},{18,2},{3,19},{19,3},{4,20},{20... | collective-permute-start | bytes 4616 | tf_op jit(solution)/shard_map/ppermute | solution.py:678
  15.5 2.6 collective-permute-start.2
  18.4 5.7 %collective-permute-done.6.refs_3_ = bf16[128,1280]{1,0:T(8,128)(2,1)} collective-permute-done((bf16[128,1280]{1,0:T(8,128)(2,1)}, bf16[128,1280]{1,0:T(8,128)(2,1)}, u32[]{:S(2)}, u32[]{:S(2)}) %collective-permute-start.6) | collective-permute-done | bytes 327712 | tf_op jit(solution)/shard_map/ppermute | solution.py:678
  24.1 3.7 %collective-permute-start.3 = (bf16[56,1280]{1,0:T(8,128)(2,1)}, bf16[56,1280]{1,0:T(8,128)(2,1)S(1)}, u32[]{:S(2)}, u32[]{:S(2)}) collective-permute-start(bf16[56,1280]{1,0:T(8,128)(2,1)} %copy-done.15), channel_id=1, source_target_pairs={{0,12},{4,0},{8,4},{12,8},{1,13},{5,1},{9,5},{13,9},{2,14},{6,2},{... | collective-permute-start | bytes 430088 | tf_op jit(solution)/shard_map/ppermute | solution.py:683
  28.5 3.3 %collective-permute-done.3.refs_9_ = bf16[56,1280]{1,0:T(8,128)(2,1)S(1)} collective-permute-done((bf16[56,1280]{1,0:T(8,128)(2,1)}, bf16[56,1280]{1,0:T(8,128)(2,1)S(1)}, u32[]{:S(2)}, u32[]{:S(2)}) %collective-permute-start.3) | collective-permute-done | bytes 143392 | tf_op jit(solution)/shard_map/ppermute | solution.py:683
  35.4 3.4 %collective-permute-start.11 = (bf16[56,1280]{1,0:T(8,128)(2,1)S(1)}, bf16[56,1280]{1,0:T(8,128)(2,1)S(1)}, u32[]{:S(2)}, u32[]{:S(2)}) collective-permute-start(bf16[56,1280]{1,0:T(8,128)(2,1)S(1)} %get-tuple-element.93), channel_id=1, source_target_pairs={{0,4},{4,8},{8,12},{12,0},{1,5},{5,9},{9,13},{13,1},{2,6},{6,10},{... | collective-permute-start | bytes 430088 | tf_op jit(solution)/shard_map/ppermute | solution.py:683
  39.2 9.0 %collective-permute-done.10.refs_4_ = bf16[56,1280]{1,0:T(8,128)(2,1)S(1)} collective-permute-done((bf16[56,1280]{1,0:T(8,128)(2,1)S(1)}, bf16[56,1280]{1,0:T(8,128)(2,1)S(1)}, u32[]{:S(2)}, u32[]{:S(2)}) %collective-permute-start.10) | collective-permute-done | bytes 143392 | tf_op jit(solution)/shard_map/ppermute | solution.py:683
  53.8 2.9 %collective-permute-start.17 = (bf16[56,1280]{1,0:T(8,128)(2,1)}, bf16[56,1280]{1,0:T(8,128)(2,1)}, u32[]{:S(2)}, u32[]{:S(2)}) collective-permute-start(bf16[56,1280]{1,0:T(8,128)(2,1)} %get-tuple-element.100), channel_id=1, source_target_pairs={{0,12},{4,0},{8,4},{12,8},{1,13},{5,1},{9,5},{13,9},{2,14},{6,2},{... | collective-permute-start | bytes 430088 | tf_op jit(solution)/shard_map/ppermute | solution.py:683
  57.7 4.4 %collective-permute-done.12.refs_1_ = s32[4,14]{1,0:T(4,128)S(1)} collective-permute-done((s32[4,14]{1,0:T(4,128)S(1)}, s32[4,14]{1,0:T(4,128)S(1)}, u32[]{:S(2)}, u32[]{:S(2)}) %collective-permute-start.12) | collective-permute-done | bytes 256 | tf_op jit(solution)/shard_map/ppermute | solution.py:683
  62.2 4.8 %collective-permute-start.14 = (s32[4,14]{1,0:T(4,128)S(1)}, s32[4,14]{1,0:T(4,128)S(1)}, u32[]{:S(2)}, u32[]{:S(2)}) collective-permute-start(s32[4,14]{1,0:T(4,128)S(1)} %pad_add_fusion.refs_0_), channel_id=1, source_target_pairs={{0,4},{4,8},{8,12},{12,0},{1,5},{5,9},{9,13},{13,1},{2,6},{6,10},{... | collective-permute-start | bytes 680 | tf_op jit(solution)/shard_map/ppermute | solution.py:683
  68.3 2.4 copy-done.1
  78.7 3.6 %collective-permute-done.18.refs_3_ = bf16[56,1280]{1,0:T(8,128)(2,1)S(1)} collective-permute-done((bf16[56,1280]{1,0:T(8,128)(2,1)S(1)}, bf16[56,1280]{1,0:T(8,128)(2,1)S(1)}, u32[]{:S(2)}, u32[]{:S(2)}) %collective-permute-start.18) | collective-permute-done | bytes 143392 | tf_op jit(solution)/shard_map/ppermute | solution.py:683
  82.3 6.6 %collective-permute-done.19.refs_4_ = bf16[56,1280]{1,0:T(8,128)(2,1)S(1)} collective-permute-done((bf16[56,1280]{1,0:T(8,128)(2,1)S(1)}, bf16[56,1280]{1,0:T(8,128)(2,1)S(1)}, u32[]{:S(2)}, u32[]{:S(2)}) %collective-permute-start.19) | collective-permute-done | bytes 143392 | tf_op jit(solution)/shard_map/ppermute | solution.py:683
  91.3 4.6 %collective-permute-start.23 = (bf16[192,1280]{1,0:T(8,128)(2,1)S(1)}, bf16[192,1280]{1,0:T(8,128)(2,1)S(1)}, u32[]{:S(2)}, u32[]{:S(2)}) collective-permute-start(bf16[192,1280]{1,0:T(8,128)(2,1)S(1)} %shard_map.136.refs_0_), channel_id=1, source_target_pairs={{0,4},{4,8},{8,12},{1,5},{5,9},{9,13},{2,6},{6,10},{10,14},{3,7},{... | collective-permute-start | bytes 1474568 | tf_op jit(solution)/shard_map/ppermute | solution.py:692
  95.9 7.1 %collective-permute-done.21.refs_1_.refs_4_ = bf16[192,1280]{1,0:T(8,128)(2,1)S(1)} collective-permute-done((bf16[192,1280]{1,0:T(8,128)(2,1)S(1)}, bf16[192,1280]{1,0:T(8,128)(2,1)S(1)}, u32[]{:S(2)}, u32[]{:S(2)}) %collective-permute-start.21) | collective-permute-done | bytes 491552 | tf_op jit(solution)/shard_map/ppermute | solution.py:691
  105.0 2.4 copy-done.2
  107.4 3.4 %shard_map.137 = (f32[2048,384]{1,0:T(8,128)S(1)}, bf16[384,1280]{1,0:T(8,128)(2,1)S(1)}, f32[2,16,192]{2,1,0:T(8,128)S(1)}) custom-call(s32[1]{0:T(128)} %bitcast.member_ref, bf16[2000,1280]{1,0:T(8,128)(2,1)S(1)} %bitcast.49, bf16[256,1280]{1,0:T(8,128)(2,1)S(1)} %get-tuple-element.102.label_ref, bf16[192,1280]{1,0:T(8,128)(2,1)S(1)} %shard_map.136.refs_0_, ...), custom_call_target="tpu_custom_call" | custom-call | flops 2013265920 | tf_op jit(solution)/shard_map/pallas_call | solution.py:388
  110.9 5.7 %collective-permute-done.22.refs_0_ = bf16[192,1280]{1,0:T(8,128)(2,1)S(1)} collective-permute-done((bf16[192,1280]{1,0:T(8,128)(2,1)S(1)}, bf16[192,1280]{1,0:T(8,128)(2,1)S(1)}, u32[]{:S(2)}, u32[]{:S(2)}) %collective-permute-start.22) | collective-permute-done | bytes 491552 | tf_op jit(solution)/shard_map/ppermute | solution.py:698
  118.5 10.9 %collective-permute-done.25.refs_2_ = bf16[192,1280]{1,0:T(8,128)(2,1)S(1)} collective-permute-done((bf16[192,1280]{1,0:T(8,128)(2,1)S(1)}, bf16[192,1280]{1,0:T(8,128)(2,1)S(1)}, u32[]{:S(2)}, u32[]{:S(2)}) %collective-permute-start.25) | collective-permute-done | bytes 491552 | tf_op jit(solution)/shard_map/ppermute | solution.py:705
  129.4 3.3 %shard_map.138 = (f32[2048,384]{1,0:T(8,128)S(1)}, bf16[384,1280]{1,0:T(8,128)(2,1)S(1)}, f32[4,16,192]{2,1,0:T(8,128)S(1)}) custom-call(s32[1]{0:T(128)} %bitcast.member_ref, bf16[2000,1280]{1,0:T(8,128)(2,1)S(1)} %bitcast.50, bf16[256,1280]{1,0:T(8,128)(2,1)S(1)} %get-tuple-element.102.label_ref, bf16[192,1280]{1,0:T(8,128)(2,1)S(1)} %collective-permute-done.22.refs_0_, ...), custom_call_target="tpu_custom_call" | custom-call | flops 2013265920 | tf_op jit(solution)/shard_map/pallas_call | solution.py:388
  132.7 5.3 %collective-permute-start.27 = (f32[4,16,192]{2,1,0:T(8,128)S(1)}, f32[4,16,192]{2,1,0:T(8,128)S(1)}, u32[]{:S(2)}, u32[]{:S(2)}) collective-permute-start(f32[4,16,192]{2,1,0:T(8,128)S(1)} %get-tuple-element.118.refs_0_), channel_id=1, source_target_pairs={{0,12},{4,0},{8,4},{12,8},{1,13},{5,1},{9,5},{13,9},{2,14},{6,2},{... | collective-permute-start | bytes 147464 | tf_op jit(solution)/shard_map/ppermute | solution.py:683
  139.9 3.3 %collective-permute-done.28.refs_2_ = f32[4,16,192]{2,1,0:T(8,128)S(1)} collective-permute-done((f32[4,16,192]{2,1,0:T(8,128)S(1)}, f32[4,16,192]{2,1,0:T(8,128)S(1)}, u32[]{:S(2)}, u32[]{:S(2)}) %collective-permute-start.28) | collective-permute-done | bytes 49184 | tf_op jit(solution)/shard_map/ppermute | solution.py:683
  144.1 6.6 %shard_map.139 = (f32[16,768]{1,0:T(8,128)S(1)}, bf16[256,768]{1,0:T(8,128)(2,1)S(1)}, bf16[256,768]{1,0:T(8,128)(2,1)S(1)}, f32[4,1]{1,0:T(4,128)S(1)}) custom-call(s32[16]{0:T(128)S(1)} %fusion.slots_ref, s32[16,128]{1,0:T(8,128)S(1)} %get-tuple-element.96.notes_ref, f32[4,16,192]{2,1,0:T(8,128)S(1)} %get-tuple-element.118.refs_0_, ...), custom_call_target="tpu_custom_call" | custom-call | flops 67108864 | tf_op jit(solution)/shard_map/pallas_call | solution.py:572
  150.7 2.8 %shard_map.142 = bf16[512,1280]{1,0:T(8,128)(2,1)S(1)} custom-call(s32[2]{0:T(128)S(1)} %get-tuple-element.135.order_ref, f32[2048,384]{1,0:T(8,128)S(1)} %get-tuple-element.124.refs_0_, f32[2048,384]{1,0:T(8,128)S(1)} %get-tuple-element.125.refs_1_, bf16[384,1280]{1,0:T(8,128)(2,1)S(1)} %get-tuple-element.126.refs_2_, ...), custom_call_target="tpu_custom_call" | custom-call | flops 1409286144 | tf_op jit(solution)/shard_map/pallas_call | solution.py:623
  153.6 2.8 shard_map.140.own_ref
  156.5 4.9 %shard_map.141 = (bf16[512,1280]{1,0:T(8,128)(2,1)S(1)}, bf16[512,1280]{1,0:T(8,128)(2,1)S(1)}) custom-call(s32[4]{0:T(128)S(1)} %pad_add_fusion.3.order_ref, f32[2048,384]{1,0:T(8,128)S(1)} %get-tuple-element.124.refs_0_, f32[2048,384]{1,0:T(8,128)S(1)} %get-tuple-element.125.refs_1_, bf16[384,1280]{1,0:T(8,128)(2,1)S(1)} %get-tuple-element.126.refs_2_, ...), custom_call_target="tpu_custom_call" | custom-call | flops 2818572288 | tf_op jit(solution)/shard_map/pallas_call | solution.py:623
  166.9 6.5 %collective-permute-done.33.refs_0_ = bf16[128,1280]{1,0:T(8,128)(2,1)S(1)} collective-permute-done((bf16[128,1280]{1,0:T(8,128)(2,1)S(1)}, bf16[128,1280]{1,0:T(8,128)(2,1)S(1)}, u32[]{:S(2)}, u32[]{:S(2)}) %collective-permute-start.33) | collective-permute-done | bytes 327712 | tf_op jit(solution)/shard_map/ppermute | solution.py:678
  177.9 2.5 collective-permute-done.32.refs_0_
  181.1 5.8 %collective-permute-done.35.refs_1_ = bf16[128,1280]{1,0:T(8,128)(2,1)S(1)} collective-permute-done((bf16[128,1280]{1,0:T(8,128)(2,1)S(1)}, bf16[128,1280]{1,0:T(8,128)(2,1)S(1)}, u32[]{:S(2)}, u32[]{:S(2)}) %collective-permute-start.35) | collective-permute-done | bytes 327712 | tf_op jit(solution)/shard_map/ppermute | solution.py:678
  191.8 6.6 %collective-permute-done.38.refs_2_ = bf16[128,1280]{1,0:T(8,128)(2,1)S(1)} collective-permute-done((bf16[128,1280]{1,0:T(8,128)(2,1)S(1)}, bf16[128,1280]{1,0:T(8,128)(2,1)S(1)}, u32[]{:S(2)}, u32[]{:S(2)}) %collective-permute-start.38) | collective-permute-done | bytes 327712 | tf_op jit(solution)/shard_map/ppermute | solution.py:678
  208.2 3.5 %collective-permute-done.42.refs_6_ = bf16[128,1280]{1,0:T(8,128)(2,1)} collective-permute-done((bf16[128,1280]{1,0:T(8,128)(2,1)S(1)}, bf16[128,1280]{1,0:T(8,128)(2,1)}, u32[]{:S(2)}, u32[]{:S(2)}) %collective-permute-start.42) | collective-permute-done | bytes 327712 | tf_op jit(solution)/shard_map/ppermute | solution.py:678
  216.9 67.6 %shard_map.146 = bf16[2000,1280]{1,0:T(8,128)(2,1)} custom-call(s32[16]{0:T(128)S(1)} %stack.123.offsets_ref, bf16[128,1280]{1,0:T(8,128)(2,1)S(1)} %get-tuple-element.142.refs_0_, bf16[128,1280]{1,0:T(8,128)(2,1)S(1)} %get-tuple-element.143.refs_1_, bf16[128,1280]{1,0:T(8,128)(2,1)S(1)} %collective-permute-done.38.refs_2_, ...), custom_call_target="tpu_custom_call" | custom-call | tf_op jit(solution)/shard_map/pallas_call | solution.py:667
  (166 shorter events, 72.2 us)
Async XLA Ops:
  0.7 10.0 %collective-permute-start = (s32[8,48]{1,0:T(8,128)}, s32[8,48]{1,0:T(8,128)S(1)}, u32[]{:S(2)}, u32[]{:S(2)}) collective-permute-start(s32[8,48]{1,0:T(8,128)} %bitcast.56), channel_id=1, source_target_pairs={{0,16},{16,0},{1,17},{17,1},{2,18},{18,2},{3,19},{19,3},{4,20},{20... | collective-permute-start | bytes 4616 | tf_op jit(solution)/shard_map/ppermute | solution.py:678
  7.5 10.9 %collective-permute-start.5 = (bf16[1280,128]{1,0:T(8,128)(2,1)}, bf16[1280,128]{1,0:T(8,128)(2,1)S(1)}, u32[]{:S(2)}, u32[]{:S(2)}) collective-permute-start(bf16[1280,128]{1,0:T(8,128)(2,1)} %dynamic-slice_bitcast_fusion.1), channel_id=1, source_target_pairs={{0,16},{16,0},{1,17},{17,1},{2,18},{18,2},{3,19},{19,3},{4,20},{20... | collective-permute-start | bytes 983048 | tf_op jit(solution)/shard_map/ppermute | solution.py:678
  7.7 16.4 %collective-permute-start.6 = (bf16[128,1280]{1,0:T(8,128)(2,1)}, bf16[128,1280]{1,0:T(8,128)(2,1)}, u32[]{:S(2)}, u32[]{:S(2)}) collective-permute-start(bf16[128,1280]{1,0:T(8,128)(2,1)} %dynamic-slice_bitcast_fusion), channel_id=1, source_target_pairs={{0,16},{16,0},{1,17},{17,1},{2,18},{18,2},{3,19},{19,3},{4,20},{20... | collective-permute-start | bytes 983048 | tf_op jit(solution)/shard_map/ppermute | solution.py:678
  13.9 13.9 %collective-permute-start.1 = (bf16[56,1280]{1,0:T(8,128)(2,1)}, bf16[56,1280]{1,0:T(8,128)(2,1)S(1)}, u32[]{:S(2)}, u32[]{:S(2)}) collective-permute-start(bf16[56,1280]{1,0:T(8,128)(2,1)} %copy-done.17), channel_id=1, source_target_pairs={{0,4},{4,8},{8,12},{12,0},{1,5},{5,9},{9,13},{13,1},{2,6},{6,10},{... | collective-permute-start | bytes 430088 | tf_op jit(solution)/shard_map/ppermute | solution.py:683
  15.5 13.0 %collective-permute-start.2 = (bf16[56,1280]{1,0:T(8,128)(2,1)}, bf16[56,1280]{1,0:T(8,128)(2,1)S(1)}, u32[]{:S(2)}, u32[]{:S(2)}) collective-permute-start(bf16[56,1280]{1,0:T(8,128)(2,1)} %copy-done.16), channel_id=1, source_target_pairs={{0,8},{4,12},{8,0},{12,4},{1,9},{5,13},{9,1},{13,5},{2,10},{6,14},... | collective-permute-start | bytes 430088 | tf_op jit(solution)/shard_map/ppermute | solution.py:683
  18.4 14.0 %collective-permute-start.7 = (bf16[1280,128]{1,0:T(8,128)(2,1)S(1)}, bf16[1280,128]{1,0:T(8,128)(2,1)S(1)}, u32[]{:S(2)}, u32[]{:S(2)}) collective-permute-start(bf16[1280,128]{1,0:T(8,128)(2,1)S(1)} %collective-permute-done.5.refs_2_), channel_id=1, source_target_pairs={{0,1},{1,0},{2,3},{3,2},{4,5},{5,4},{6,7},{7,6},{8,9},{9,8},{10,11... | collective-permute-start | bytes 983048 | tf_op jit(solution)/shard_map/ppermute | solution.py:678
  34.6 13.6 %collective-permute-start.10 = (bf16[56,1280]{1,0:T(8,128)(2,1)S(1)}, bf16[56,1280]{1,0:T(8,128)(2,1)S(1)}, u32[]{:S(2)}, u32[]{:S(2)}) collective-permute-start(bf16[56,1280]{1,0:T(8,128)(2,1)S(1)} %get-tuple-element.92), channel_id=1, source_target_pairs={{0,8},{4,12},{8,0},{12,4},{1,9},{5,13},{9,1},{13,5},{2,10},{6,14},... | collective-permute-start | bytes 430088 | tf_op jit(solution)/shard_map/ppermute | solution.py:683
  35.4 12.8 %collective-permute-start.11 = (bf16[56,1280]{1,0:T(8,128)(2,1)S(1)}, bf16[56,1280]{1,0:T(8,128)(2,1)S(1)}, u32[]{:S(2)}, u32[]{:S(2)}) collective-permute-start(bf16[56,1280]{1,0:T(8,128)(2,1)S(1)} %get-tuple-element.93), channel_id=1, source_target_pairs={{0,4},{4,8},{8,12},{12,0},{1,5},{5,9},{9,13},{13,1},{2,6},{6,10},{... | collective-permute-start | bytes 430088 | tf_op jit(solution)/shard_map/ppermute | solution.py:683
  38.8 9.7 %collective-permute-start.9 = (bf16[56,1280]{1,0:T(8,128)(2,1)S(1)}, bf16[56,1280]{1,0:T(8,128)(2,1)S(1)}, u32[]{:S(2)}, u32[]{:S(2)}) collective-permute-start(bf16[56,1280]{1,0:T(8,128)(2,1)S(1)} %get-tuple-element.91), channel_id=1, source_target_pairs={{0,12},{4,0},{8,4},{12,8},{1,13},{5,1},{9,5},{13,9},{2,14},{6,2},{... | collective-permute-start | bytes 430088 | tf_op jit(solution)/shard_map/ppermute | solution.py:683
  51.3 21.3 %collective-permute-start.15 = (bf16[56,1280]{1,0:T(8,128)(2,1)}, bf16[56,1280]{1,0:T(8,128)(2,1)S(1)}, u32[]{:S(2)}, u32[]{:S(2)}) collective-permute-start(bf16[56,1280]{1,0:T(8,128)(2,1)} %get-tuple-element.98), channel_id=1, source_target_pairs={{0,4},{4,8},{8,12},{12,0},{1,5},{5,9},{9,13},{13,1},{2,6},{6,10},{... | collective-permute-start | bytes 430088 | tf_op jit(solution)/shard_map/ppermute | solution.py:683
  53.3 19.3 %collective-permute-start.16 = (bf16[56,1280]{1,0:T(8,128)(2,1)}, bf16[56,1280]{1,0:T(8,128)(2,1)}, u32[]{:S(2)}, u32[]{:S(2)}) collective-permute-start(bf16[56,1280]{1,0:T(8,128)(2,1)} %get-tuple-element.99), channel_id=1, source_target_pairs={{0,8},{4,12},{8,0},{12,4},{1,9},{5,13},{9,1},{13,5},{2,10},{6,14},... | collective-permute-start | bytes 430088 | tf_op jit(solution)/shard_map/ppermute | solution.py:683
  53.8 18.8 %collective-permute-start.17 = (bf16[56,1280]{1,0:T(8,128)(2,1)}, bf16[56,1280]{1,0:T(8,128)(2,1)}, u32[]{:S(2)}, u32[]{:S(2)}) collective-permute-start(bf16[56,1280]{1,0:T(8,128)(2,1)} %get-tuple-element.100), channel_id=1, source_target_pairs={{0,12},{4,0},{8,4},{12,8},{1,13},{5,1},{9,5},{13,9},{2,14},{6,2},{... | collective-permute-start | bytes 430088 | tf_op jit(solution)/shard_map/ppermute | solution.py:683
  76.7 12.3 %collective-permute-start.19 = (bf16[56,1280]{1,0:T(8,128)(2,1)S(1)}, bf16[56,1280]{1,0:T(8,128)(2,1)S(1)}, u32[]{:S(2)}, u32[]{:S(2)}) collective-permute-start(bf16[56,1280]{1,0:T(8,128)(2,1)S(1)} %get-tuple-element.110), channel_id=1, source_target_pairs={{0,8},{4,12},{8,0},{12,4},{1,9},{5,13},{9,1},{13,5},{2,10},{6,14},... | collective-permute-start | bytes 430088 | tf_op jit(solution)/shard_map/ppermute | solution.py:683
  78.7 10.3 %collective-permute-start.20 = (bf16[56,1280]{1,0:T(8,128)(2,1)S(1)}, bf16[56,1280]{1,0:T(8,128)(2,1)S(1)}, u32[]{:S(2)}, u32[]{:S(2)}) collective-permute-start(bf16[56,1280]{1,0:T(8,128)(2,1)S(1)} %get-tuple-element.111), channel_id=1, source_target_pairs={{0,4},{4,8},{8,12},{12,0},{1,5},{5,9},{9,13},{13,1},{2,6},{6,10},{... | collective-permute-start | bytes 430088 | tf_op jit(solution)/shard_map/ppermute | solution.py:683
  90.0 13.0 %collective-permute-start.21 = (bf16[192,1280]{1,0:T(8,128)(2,1)S(1)}, bf16[192,1280]{1,0:T(8,128)(2,1)S(1)}, u32[]{:S(2)}, u32[]{:S(2)}) collective-permute-start(bf16[192,1280]{1,0:T(8,128)(2,1)S(1)} %shard_map.136.refs_0_), channel_id=1, source_target_pairs={{4,0},{8,4},{12,8},{5,1},{9,5},{13,9},{6,2},{10,6},{14,10},{7,3},{... | collective-permute-start | bytes 1474568 | tf_op jit(solution)/shard_map/ppermute | solution.py:691
  91.3 13.0 %collective-permute-start.23 = (bf16[192,1280]{1,0:T(8,128)(2,1)S(1)}, bf16[192,1280]{1,0:T(8,128)(2,1)S(1)}, u32[]{:S(2)}, u32[]{:S(2)}) collective-permute-start(bf16[192,1280]{1,0:T(8,128)(2,1)S(1)} %shard_map.136.refs_0_), channel_id=1, source_target_pairs={{0,4},{4,8},{8,12},{1,5},{5,9},{9,13},{2,6},{6,10},{10,14},{3,7},{... | collective-permute-start | bytes 1474568 | tf_op jit(solution)/shard_map/ppermute | solution.py:692
  103.0 13.6 %collective-permute-start.22 = (bf16[192,1280]{1,0:T(8,128)(2,1)S(1)}, bf16[192,1280]{1,0:T(8,128)(2,1)S(1)}, u32[]{:S(2)}, u32[]{:S(2)}) collective-permute-start(bf16[192,1280]{1,0:T(8,128)(2,1)S(1)} %collective-permute-done.21.refs_1_.refs_4_), channel_id=1, source_target_pairs={{4,0},{8,4},{5,1},{9,5},{6,2},{10,6},{7,3},{11,7},{20,16},{24,20},... | collective-permute-start | bytes 1474568 | tf_op jit(solution)/shard_map/ppermute | solution.py:698
  104.3 12.3 %collective-permute-start.24 = (bf16[192,1280]{1,0:T(8,128)(2,1)S(1)}, bf16[192,1280]{1,0:T(8,128)(2,1)S(1)}, u32[]{:S(2)}, u32[]{:S(2)}) collective-permute-start(bf16[192,1280]{1,0:T(8,128)(2,1)S(1)} %collective-permute-done.23.refs_2_.refs_5_), channel_id=1, source_target_pairs={{4,8},{8,12},{5,9},{9,13},{6,10},{10,14},{7,11},{11,15},{20,24},{2... | collective-permute-start | bytes 1474568 | tf_op jit(solution)/shard_map/ppermute | solution.py:699
  116.6 12.9 %collective-permute-start.25 = (bf16[192,1280]{1,0:T(8,128)(2,1)S(1)}, bf16[192,1280]{1,0:T(8,128)(2,1)S(1)}, u32[]{:S(2)}, u32[]{:S(2)}) collective-permute-start(bf16[192,1280]{1,0:T(8,128)(2,1)S(1)} %collective-permute-done.22.refs_0_), channel_id=1, source_target_pairs={{4,0},{5,1},{6,2},{7,3},{20,16},{21,17},{22,18},{23,19}} | collective-permute-start | bytes 1474568 | tf_op jit(solution)/shard_map/ppermute | solution.py:705
  117.8 11.6 %collective-permute-start.26 = (bf16[192,1280]{1,0:T(8,128)(2,1)S(1)}, bf16[192,1280]{1,0:T(8,128)(2,1)S(1)}, u32[]{:S(2)}, u32[]{:S(2)}) collective-permute-start(bf16[192,1280]{1,0:T(8,128)(2,1)S(1)} %collective-permute-done.24.refs_1_), channel_id=1, source_target_pairs={{8,12},{9,13},{10,14},{11,15},{24,28},{25,29},{26,30},{27,31}} | collective-permute-start | bytes 1474568 | tf_op jit(solution)/shard_map/ppermute | solution.py:706
  162.8 10.6 %collective-permute-start.33 = (bf16[128,1280]{1,0:T(8,128)(2,1)S(1)}, bf16[128,1280]{1,0:T(8,128)(2,1)S(1)}, u32[]{:S(2)}, u32[]{:S(2)}) collective-permute-start(bf16[128,1280]{1,0:T(8,128)(2,1)S(1)} %get-tuple-element.137), channel_id=1, source_target_pairs={{0,16},{16,0},{1,17},{17,1},{2,18},{18,2},{3,19},{19,3},{4,20},{20... | collective-permute-start | bytes 983048 | tf_op jit(solution)/shard_map/ppermute | solution.py:678
  163.4 10.6 %collective-permute-start.34 = (bf16[128,1280]{1,0:T(8,128)(2,1)S(1)}, bf16[128,1280]{1,0:T(8,128)(2,1)S(1)}, u32[]{:S(2)}, u32[]{:S(2)}) collective-permute-start(bf16[128,1280]{1,0:T(8,128)(2,1)S(1)} %get-tuple-element.138), channel_id=1, source_target_pairs={{0,2},{2,0},{1,3},{3,1},{4,6},{6,4},{5,7},{7,5},{8,10},{10,8},{9,1... | collective-permute-start | bytes 983048 | tf_op jit(solution)/shard_map/ppermute | solution.py:678
  164.9 15.5 %collective-permute-start.32 = (bf16[128,1280]{1,0:T(8,128)(2,1)S(1)}, bf16[128,1280]{1,0:T(8,128)(2,1)S(1)}, u32[]{:S(2)}, u32[]{:S(2)}) collective-permute-start(bf16[128,1280]{1,0:T(8,128)(2,1)S(1)} %get-tuple-element.136), channel_id=1, source_target_pairs={{0,16},{16,0},{1,17},{17,1},{2,18},{18,2},{3,19},{19,3},{4,20},{20... | collective-permute-start | bytes 983048 | tf_op jit(solution)/shard_map/ppermute | solution.py:678
  166.4 14.6 %collective-permute-start.36 = (bf16[128,1280]{1,0:T(8,128)(2,1)S(1)}, bf16[128,1280]{1,0:T(8,128)(2,1)S(1)}, u32[]{:S(2)}, u32[]{:S(2)}) collective-permute-start(bf16[128,1280]{1,0:T(8,128)(2,1)S(1)} %get-tuple-element.140), channel_id=1, source_target_pairs={{0,2},{2,0},{1,3},{3,1},{4,6},{6,4},{5,7},{7,5},{8,10},{10,8},{9,1... | collective-permute-start | bytes 983048 | tf_op jit(solution)/shard_map/ppermute | solution.py:678
  174.8 12.0 %collective-permute-start.35 = (bf16[128,1280]{1,0:T(8,128)(2,1)S(1)}, bf16[128,1280]{1,0:T(8,128)(2,1)S(1)}, u32[]{:S(2)}, u32[]{:S(2)}) collective-permute-start(bf16[128,1280]{1,0:T(8,128)(2,1)S(1)} %get-tuple-element.139), channel_id=1, source_target_pairs={{0,2},{2,0},{1,3},{3,1},{4,6},{6,4},{5,7},{7,5},{8,10},{10,8},{9,1... | collective-permute-start | bytes 983048 | tf_op jit(solution)/shard_map/ppermute | solution.py:678
  176.4 10.4 %collective-permute-start.37 = (bf16[128,1280]{1,0:T(8,128)(2,1)S(1)}, bf16[128,1280]{1,0:T(8,128)(2,1)S(1)}, u32[]{:S(2)}, u32[]{:S(2)}) collective-permute-start(bf16[128,1280]{1,0:T(8,128)(2,1)S(1)} %get-tuple-element.141), channel_id=1, source_target_pairs={{0,16},{16,0},{1,17},{17,1},{2,18},{18,2},{3,19},{19,3},{4,20},{20... | collective-permute-start | bytes 983048 | tf_op jit(solution)/shard_map/ppermute | solution.py:678
  187.7 10.7 %collective-permute-start.38 = (bf16[128,1280]{1,0:T(8,128)(2,1)S(1)}, bf16[128,1280]{1,0:T(8,128)(2,1)S(1)}, u32[]{:S(2)}, u32[]{:S(2)}) collective-permute-start(bf16[128,1280]{1,0:T(8,128)(2,1)S(1)} %get-tuple-element.142.refs_0_), channel_id=1, source_target_pairs={{0,2},{2,0},{1,3},{3,1},{4,6},{6,4},{5,7},{7,5},{8,10},{10,8},{9,1... | collective-permute-start | bytes 983048 | tf_op jit(solution)/shard_map/ppermute | solution.py:678
  189.3 10.6 %collective-permute-start.41 = (bf16[128,1280]{1,0:T(8,128)(2,1)S(1)}, bf16[128,1280]{1,0:T(8,128)(2,1)S(1)}, u32[]{:S(2)}, u32[]{:S(2)}) collective-permute-start(bf16[128,1280]{1,0:T(8,128)(2,1)S(1)} %get-tuple-element.143.refs_1_), channel_id=1, source_target_pairs={{0,16},{16,0},{1,17},{17,1},{2,18},{18,2},{3,19},{19,3},{4,20},{20... | collective-permute-start | bytes 983048 | tf_op jit(solution)/shard_map/ppermute | solution.py:678
  190.8 12.5 %collective-permute-start.39 = (bf16[128,1280]{1,0:T(8,128)(2,1)S(1)}, bf16[128,1280]{1,0:T(8,128)(2,1)S(1)}, u32[]{:S(2)}, u32[]{:S(2)}) collective-permute-start(bf16[128,1280]{1,0:T(8,128)(2,1)S(1)} %get-tuple-element.143.refs_1_), channel_id=1, source_target_pairs={{0,2},{2,0},{1,3},{3,1},{4,6},{6,4},{5,7},{7,5},{8,10},{10,8},{9,1... | collective-permute-start | bytes 983048 | tf_op jit(solution)/shard_map/ppermute | solution.py:678
  191.3 15.7 %collective-permute-start.40 = (bf16[128,1280]{1,0:T(8,128)(2,1)S(1)}, bf16[128,1280]{1,0:T(8,128)(2,1)S(1)}, u32[]{:S(2)}, u32[]{:S(2)}) collective-permute-start(bf16[128,1280]{1,0:T(8,128)(2,1)S(1)} %get-tuple-element.142.refs_0_), channel_id=1, source_target_pairs={{0,16},{16,0},{1,17},{17,1},{2,18},{18,2},{3,19},{19,3},{4,20},{20... | collective-permute-start | bytes 983048 | tf_op jit(solution)/shard_map/ppermute | solution.py:678
  191.8 15.1 %collective-permute-start.44 = (bf16[128,1280]{1,0:T(8,128)(2,1)S(1)}, bf16[128,1280]{1,0:T(8,128)(2,1)S(1)}, u32[]{:S(2)}, u32[]{:S(2)}) collective-permute-start(bf16[128,1280]{1,0:T(8,128)(2,1)S(1)} %get-tuple-element.142.refs_0_), channel_id=1, source_target_pairs={{0,1},{1,0},{2,3},{3,2},{4,5},{5,4},{6,7},{7,6},{8,9},{9,8},{10,11... | collective-permute-start | bytes 983048 | tf_op jit(solution)/shard_map/ppermute | solution.py:678
  199.9 11.8 %collective-permute-start.42 = (bf16[128,1280]{1,0:T(8,128)(2,1)S(1)}, bf16[128,1280]{1,0:T(8,128)(2,1)}, u32[]{:S(2)}, u32[]{:S(2)}) collective-permute-start(bf16[128,1280]{1,0:T(8,128)(2,1)S(1)} %collective-permute-done.38.refs_2_), channel_id=1, source_target_pairs={{0,16},{16,0},{1,17},{17,1},{2,18},{18,2},{3,19},{19,3},{4,20},{20... | collective-permute-start | bytes 983048 | tf_op jit(solution)/shard_map/ppermute | solution.py:678
  (45 other events, 283.7 us)
